TPU v7x, 256 devices: a whole 4x4x8 slice. The times are simulated.
256 devices in a mesh: dp: 8 (over x, y_lo), mp: 32 (over y_hi, z, core).
Axes of the slice: x: 4, y: 4 (y_hi: 2, y_lo: 2; y = y_hi * 2 + y_lo), z: 8, core: 2. Of those that a mesh axis runs over, the one named last changes fastest.
Arguments:
- block_in: bfloat16 [2048, 6144], P(('dp', 'mp')), may hold values from -6 to 6
- norm_gain: float32 [6144], replicated, may hold values from 0.5 to 1.5
- weight_in: bfloat16 [6144, 12288], P(None, 'mp'), may hold values from -0.078125 to 0.078125
- weight_out: bfloat16 [12288, 6144], P('mp'), may hold values from -0.0546875 to 0.0546875
- output_grad: bfloat16 [2048, 6144], P(('dp', 'mp')), may hold values from -24 to 24
Outputs:
- mixed: bfloat16 [2048, 6144], P(('dp', 'mp'))
- input_grad: bfloat16 [2048, 6144], P(('dp', 'mp'))
- grad_in: float32 [6144, 12288], P('dp', 'mp')
- grad_out: float32 [12288, 6144], P('mp', 'dp')
All inputs are finite; a program needn't handle non-finite values.
Results may differ from a plain program's by a relative error of at most 0.02.
Values may be sent and summed in bfloat16 or wider, within the bound.
A program may use at most 128 MiB of HBM per device.

v0:
```python
import jax
import jax.numpy as jnp
from jax import lax
from jax.sharding import PartitionSpec as P


def normal_cdf(value):
    return 0.5 * (1.0 + lax.erf(value * 0.7071067811865476))


def contract_rows(left, right):
    return lax.dot_general(
        left, right, (((0,), (0,)), ((), ())), preferred_element_type=jnp.float32
    )


def local(block_in, norm_gain, weight_in, weight_out, output_grad):
    values = block_in.astype(jnp.float32)
    average = jnp.mean(values, axis=1, keepdims=True)
    centred = values - average
    inv_scale = lax.rsqrt(jnp.mean(centred * centred, axis=1, keepdims=True) + 1e-06)
    standard = centred * inv_scale
    normed = (standard * norm_gain).astype(jnp.bfloat16)
    normed_all = lax.all_gather(normed, "mp", axis=0, tiled=True)
    preact = jnp.dot(normed_all, weight_in, preferred_element_type=jnp.float32)
    hidden = (preact * normal_cdf(preact)).astype(jnp.bfloat16)
    block = hidden
    branch = lax.psum_scatter(
        jnp.dot(block, weight_out, preferred_element_type=jnp.float32).astype(jnp.bfloat16),
        "mp",
        scatter_dimension=0,
        tiled=True,
    ).astype(jnp.float32)
    mixed = (values + branch).astype(jnp.bfloat16)
    grad_all = lax.all_gather(output_grad, "mp", axis=0, tiled=True)
    hidden_grad = lax.dot_general(
        grad_all, weight_out, (((1,), (1,)), ((), ())), preferred_element_type=jnp.float32
    )
    slope = normal_cdf(preact) + preact * jnp.exp(-0.5 * preact * preact) * 0.3989422804014327
    preact_grad = (hidden_grad * slope).astype(jnp.bfloat16)
    block = preact_grad
    normed_grad = lax.psum_scatter(
        lax.dot_general(
            block, weight_in, (((1,), (1,)), ((), ())), preferred_element_type=jnp.float32
        ).astype(jnp.bfloat16),
        "mp",
        scatter_dimension=0,
        tiled=True,
    ).astype(jnp.float32)
    scaled = normed_grad * norm_gain
    input_grad = output_grad.astype(jnp.float32) + inv_scale * (
        scaled
        - jnp.mean(scaled, axis=1, keepdims=True)
        - standard * jnp.mean(scaled * standard, axis=1, keepdims=True)
    )
    input_grad = input_grad.astype(jnp.bfloat16)
    term_in = contract_rows(normed_all, preact_grad)
    term_out = contract_rows(hidden, grad_all)
    grad_in, grad_out = (
        lax.psum_scatter(
            term_in.astype(jnp.bfloat16), "dp", scatter_dimension=0, tiled=True
        ).astype(jnp.float32),
        lax.psum_scatter(
            term_out.astype(jnp.bfloat16), "dp", scatter_dimension=1, tiled=True
        ).astype(jnp.float32),
    )
    return (mixed, input_grad, grad_in, grad_out)


def solution(mesh):
    in_specs = (P(("dp", "mp"), None), P(), P(None, "mp"), P("mp", None), P(("dp", "mp"), None))
    out_specs = (P(("dp", "mp"), None), P(("dp", "mp"), None), P("dp", "mp"), P("mp", "dp"))
    return jax.shard_map(local, mesh=mesh, in_specs=in_specs, out_specs=out_specs, check_vma=False)
```

profile of v0, /device:TPU:1, one launch (start us, length us, event | category | flops | bytes accessed | tf_op | source)
XLA Modules:
  0.0 654.4 jit_solution(9751874968804197483)
XLA Ops:
  7.2 0.0 all-gather.3.cloned.1.call-start
  7.2 1.1 convert_reduce_fusion
  8.3 1.1 fusion.16
  9.4 1.6 fusion.10
  11.0 0.0 all-gather.3.cloned.1.call-update
  11.1 0.0 all-gather.5.cloned.1.call-start
  11.1 0.7 all-gather.5.cloned.1.call-update
  11.8 0.0 reduce-scatter.7.cloned.1.call-start
  11.9 86.9 %all-gather.3.cloned.1.call-done = bf16[256,6144]{1,0:T(8,128)(2,1)} async-done(((bf16[8,6144]{1,0:T(8,128)(2,1)}), bf16[256,6144]{1,0:T(8,128)(2,1)}) %all-gather.3.cloned.1.call-update) | async-done | bytes 3145744 | tf_op jit(solution)/shard_map/all_gather | solution.py:24
  98.8 5.1 fusion.19
  103.9 0.0 copy-start.3
  103.9 77.7 %all-gather.5.cloned.1.call-done = bf16[256,6144]{1,0:T(8,128)(2,1)} async-done(((bf16[8,6144]{1,0:T(8,128)(2,1)}), bf16[256,6144]{1,0:T(8,128)(2,1)}) %all-gather.5.cloned.1.call-update) | async-done | bytes 3145744 | tf_op jit(solution)/shard_map/all_gather | solution.py:35
  181.6 5.2 fusion
  186.8 3.5 convolution_convert_fusion.2
  190.4 0.0 reduce-scatter.7.cloned.1.call-update
  190.4 0.0 reduce-scatter.5.cloned.1.call-start
  190.4 5.8 convolution_convert_fusion.3
  196.2 0.0 reduce-scatter.5.cloned.1.call-update
  196.3 0.0 reduce-scatter.11.cloned.1.call-start
  196.3 5.8 convolution_convert_fusion
  202.1 0.0 reduce-scatter.11.cloned.1.call-update
  202.1 0.0 reduce-scatter.9.cloned.1.call-start
  202.2 4.0 convolution_convert_fusion.1
  206.2 0.0 reduce-scatter.9.cloned.1.call-update
  206.2 98.9 %reduce-scatter.7.cloned.1.call-done = bf16[8,6144]{1,0:T(8,128)(2,1)} async-done(((bf16[256,6144]{1,0:T(8,128)(2,1)}), bf16[8,6144]{1,0:T(8,128)(2,1)}) %reduce-scatter.7.cloned.1.call-update) | async-done | bytes 98320 | tf_op jit(solution)/shard_map/reduce_scatter | solution.py:42
  305.1 1.2 fusion.18
  306.3 124.8 %reduce-scatter.5.cloned.1.call-done = bf16[8,6144]{1,0:T(8,128)(2,1)} async-done(((bf16[256,6144]{1,0:T(8,128)(2,1)}), bf16[8,6144]{1,0:T(8,128)(2,1)}) %reduce-scatter.5.cloned.1.call-update) | async-done | bytes 98320 | tf_op jit(solution)/shard_map/reduce_scatter | solution.py:28
  431.1 1.7 fusion.15
  432.8 106.5 %reduce-scatter.11.cloned.1.call-done = bf16[384,768]{1,0:T(8,128)(2,1)} async-done(((bf16[384,6144]{1,0:T(8,128)(2,1)}), bf16[384,768]{1,0:T(8,128)(2,1)}) %reduce-scatter.11.cloned.1.call-update) | async-done | bytes 589840 | tf_op jit(solution)/shard_map/reduce_scatter | solution.py:63
  539.3 2.2 convert_element_type.59
  541.4 103.9 %reduce-scatter.9.cloned.1.call-done = bf16[768,384]{1,0:T(8,128)(2,1)} async-done(((bf16[6144,384]{1,0:T(8,128)(2,1)}), bf16[768,384]{1,0:T(8,128)(2,1)}) %reduce-scatter.9.cloned.1.call-update) | async-done | bytes 589840 | tf_op jit(solution)/shard_map/reduce_scatter | solution.py:60
  645.4 2.2 convert_element_type.57
  (14 shorter events, 0.0 us)
Async XLA Ops:
  7.2 91.6 %all-gather.3.cloned.1.call-start = ((), (), s32[]{:S(2)}) async-start(), calls=%async_computation.4 | async-start | bytes 3244032 | tf_op jit(solution)/shard_map/all_gather | solution.py:24
  11.1 170.5 %all-gather.5.cloned.1.call-start = ((), (), s32[]{:S(2)}) async-start(), calls=%async_computation.6 | async-start | bytes 3244032 | tf_op jit(solution)/shard_map/all_gather | solution.py:35
  11.8 293.3 %reduce-scatter.7.cloned.1.call-start = ((), (), s32[]{:S(2)}) async-start(), calls=%async_computation.7 | async-start | bytes 3244032 | tf_op jit(solution)/shard_map/reduce_scatter | solution.py:42
  103.9 86.5 %copy-start.3 = (f32[256,384]{1,0:T(8,128)}, f32[256,384]{1,0:T(8,128)S(1)}, u32[]{:S(2)}) copy-start(f32[256,384]{1,0:T(8,128)S(1)} %fusion.19) | copy-start | bytes 1179652
  181.6 5.3 copy-start.1
  190.4 240.7 %reduce-scatter.5.cloned.1.call-start = ((), (), s32[]{:S(2)}) async-start(), calls=%async_computation.5 | async-start | bytes 3244032 | tf_op jit(solution)/shard_map/reduce_scatter | solution.py:28
  196.3 5.9 copy-start
  196.3 343.0 %reduce-scatter.11.cloned.1.call-start = ((), (), s32[]{:S(2)}) async-start(), calls=%async_computation.9 | async-start | bytes 5308416 | tf_op jit(solution)/shard_map/reduce_scatter | solution.py:63
  202.1 443.2 %reduce-scatter.9.cloned.1.call-start = ((), (), s32[]{:S(2)}) async-start(), calls=%async_computation.8 | async-start | bytes 5308416 | tf_op jit(solution)/shard_map/reduce_scatter | solution.py:60
  206.2 98.9 %copy-start.2 = (bf16[8,6144]{1,0:T(8,128)(2,1)S(1)}, bf16[8,6144]{1,0:T(8,128)(2,1)}, u32[]{:S(2)}) copy-start(bf16[8,6144]{1,0:T(8,128)(2,1)} %param.5) | copy-start | bytes 294916
  206.2 98.9 %copy-start.5 = (f32[6144]{0:T(1024)S(1)}, f32[6144]{0:T(1024)}, u32[]{:S(2)}) copy-start(f32[6144]{0:T(1024)} %param.6) | copy-start | bytes 73732
  206.2 224.9 %copy-start.4 = (bf16[8,6144]{1,0:T(8,128)(2,1)S(1)}, bf16[8,6144]{1,0:T(8,128)(2,1)}, u32[]{:S(2)}) copy-start(bf16[8,6144]{1,0:T(8,128)(2,1)} %param.9) | copy-start | bytes 294916
Sparse Core Ops, SparseCore 0:
  11.3 87.4 all-gather.2
  101.6 79.9 all-gather.4
  190.5 114.5 reduce-scatter.6
  309.7 121.3 reduce-scatter.4
  433.5 105.7 reduce-scatter.10
  541.7 103.6 reduce-scatter.8
where the time goes:
time: 655 us; the launch traced here: 654 us
  waiting for transfers between devices  599 us (91%)
  matrix products  29.4 us (4%)
  between operations  14.2 us (2%)
  other arithmetic  11 us (2%)
    reduce_scatter x1, waiting for transfers between devices, local(): lax.psum_scatter(jnp.dot(block, weight_out, preferred_element_type=jnp.fl...  125 us
    reduce_scatter x1, waiting for transfers between devices, local(): lax.psum_scatter(term_out.astype(jnp.bfloat16), 'dp', scatter_dimension=1...  106 us
    reduce_scatter x1, waiting for transfers between devices, local(): lax.psum_scatter(term_in.astype(jnp.bfloat16), 'dp', scatter_dimension=0,...  104 us
    reduce_scatter x1, waiting for transfers between devices, local(): lax.psum_scatter(lax.dot_general(block, weight_in, (((1,), (1,)), ((), ()...  98.9 us
    all_gather x1, waiting for transfers between devices, local(): normed_all = lax.all_gather(normed, 'mp', axis=0, tiled=True)  86.9 us
    all_gather x1, waiting for transfers between devices, local(): grad_all = lax.all_gather(output_grad, 'mp', axis=0, tiled=True)  77.7 us
  transfers between devices with their start and end apart: 6, of which 6 were waited for; matrix products, arithmetic and copies ran while one was open for 4% of the time, Pallas kernels for 0%

commit v1 on v0

v1 whole, which is shorter than its diff:
```python
import jax
import jax.numpy as jnp
from jax import lax
from jax.experimental import pallas as pl
from jax.experimental.pallas import tpu as pltpu
from jax.sharding import PartitionSpec as P

MESH = pl.DeviceIdType.MESH
F32, BF16 = jnp.float32, jnp.bfloat16

NX, NZ = 4, 8
ROWS = 8
CHUNK = NX * ROWS
WIDE = 1536
UNITS = 384
BLOCK = 256
SEMS = 192


def place():
    dp, mp = lax.axis_index("dp"), lax.axis_index("mp")
    return (
        lax.div(dp, 2),
        lax.rem(dp, 2),
        lax.div(mp, 16),
        lax.rem(lax.div(mp, 2), NZ),
        lax.rem(mp, 2),
    )


def device(x, yl, yh, z, c):
    return (x * 2 + yl, (yh * NZ + z) * 2 + c)


def slot(way, dist):
    if dist == 0:
        return 0
    if dist == 4:
        return 7
    return 2 * dist - 1 + way


def on_ring(way, dist, h):
    return dist < 4 or way == h


def dot(left, right, dims=((1,), (0,))):
    return lax.dot_general(left, right, (dims, ((), ())), preferred_element_type=F32)


def kernel(
    x_ref, gain_ref, wi_any, wo_any, g_ref,
    mixed_ref, igrad_ref, gin_any, gout_any,
    wi, wo, std, msg, got, acts, cots,
    part, part_in, slope, hid, dpre, hid_t, dpre_t,
    prod, prod_sib, ring_in, ring_out, y_out, y_in, rows_out, rows_in,
    gsum, gsend, gin_got, gres, gturn,
    ssem, rsem, lsem,
):
    x, yl, yh, z, c = place()
    xs = [lax.rem(x + k, NX) for k in range(NX)]
    zp, zm = lax.rem(z + 1, NZ), lax.rem(z + NZ - 1, NZ)
    to_z = (device(x, yl, yh, zp, c), device(x, yl, yh, zm, c))
    to_sib = device(x, yl, yh, z, 1 - c)
    to_yh = device(x, yl, 1 - yh, z, c)
    to_yl = device(x, 1 - yl, yh, z, c)
    to_x = [device(xs[k], yl, yh, z, c) for k in range(NX)]

    barrier = pltpu.get_barrier_semaphore()
    for other in (*to_z, to_sib, to_yh, to_yl, *to_x[1:]):
        pl.semaphore_signal(barrier, inc=1, device_id=other, device_id_type=MESH)

    load_wi = pltpu.make_async_copy(
        wi_any.at[pl.ds(pl.multiple_of(x * WIDE, WIDE), WIDE)], wi, lsem.at[0])
    load_wo = pltpu.make_async_copy(
        wo_any.at[:, pl.ds(pl.multiple_of(x * WIDE, WIDE), WIDE)], wo, lsem.at[1])
    load_wi.start()
    load_wo.start()

    values = x_ref[...].astype(F32)
    average = jnp.mean(values, axis=1, keepdims=True)
    centred = values - average
    inv_scale = lax.rsqrt(jnp.mean(centred * centred, axis=1, keepdims=True) + 1e-06)
    standard = centred * inv_scale
    std[...] = standard
    normed = standard * gain_ref[...]
    grad = g_ref[...].astype(F32)
    for q in range(NX):
        cols = slice(q * WIDE, (q + 1) * WIDE)
        msg[q] = jnp.concatenate([normed[:, cols], grad[:, cols]], axis=0).astype(BF16)

    pl.semaphore_wait(barrier, 8)

    pending = []

    def send(src, dst, to):
        k = len(pending)
        copy = pltpu.make_async_remote_copy(
            src_ref=src, dst_ref=dst, send_sem=ssem.at[k], recv_sem=rsem.at[k],
            device_id=to, device_id_type=MESH)
        copy.start()
        pending.append(copy)
        return copy

    first = [send(msg.at[xs[k]], got.at[x], to_x[k]) for k in range(1, NX)]
    got[x] = msg[x]
    for copy in first:
        copy.wait_recv()
    pieces = [got[a].astype(F32) for a in range(NX)]
    acts[0] = jnp.concatenate([p[:ROWS] for p in pieces], axis=0).astype(BF16)
    cots[0] = jnp.concatenate([p[ROWS:] for p in pieces], axis=0).astype(BF16)

    class Gather:
        def __init__(self, buf):
            self.buf, self.ring, self.sib = buf, {}, {}

        def spread(self, way, dist, h):
            s = slot(way, dist)
            k = 4 * s + 2 * h
            for w in (0, 1) if dist == 0 else (way,):
                if dist < 4 and on_ring(w, dist + 1, h):
                    t = 4 * slot(w, dist + 1) + 2 * h
                    self.ring[w, dist + 1, h] = send(self.buf.at[k], self.buf.at[t], to_z[w])
            self.sib[s, h] = send(self.buf.at[k], self.buf.at[k + 1], to_sib)

        def start(self):
            self.y = send(self.buf.at[0], self.buf.at[2], to_yh)
            self.spread(0, 0, 0)

        def other(self):
            self.y.wait_recv()
            self.spread(0, 0, 1)

        def step(self, dist):
            for h in (0, 1):
                for way in (0, 1):
                    if on_ring(way, dist, h):
                        self.ring[way, dist, h].wait_recv()
                        self.spread(way, dist, h)

        def block(self, b):
            for s in (2 * b, 2 * b + 1):
                for h in (0, 1):
                    self.sib[s, h].wait_recv()
            return self.buf[8 * b:8 * b + 8].reshape(BLOCK, WIDE)

    class Across:
        def __init__(self, i, result):
            self.part, self.came, self.result = part.at[i], part_in.at[i], result
            self.out, self.back = {}, {}

        def give(self, b, term):
            self.part[b] = term.astype(BF16).reshape(NX, BLOCK // NX, UNITS)
            self.out[b] = [
                send(self.part.at[b, xs[k]], self.came.at[b, k - 1], to_x[k]) for k in range(1, NX)]

        def total(self, b):
            for copy in self.out[b]:
                copy.wait_recv()
            total = self.part[b, x].astype(F32)
            for k in range(NX - 1):
                total = total + self.came[b, k].astype(F32)
            return total

        def share(self, b, value):
            self.result[b, x] = value.astype(BF16)
            self.back[b] = [
                send(self.result.at[b, x], self.result.at[b, x], to_x[k]) for k in range(1, NX)]

        def whole(self, b):
            for copy in self.back[b]:
                copy.wait_recv()
            return self.result[b].reshape(BLOCK, UNITS)

    class Scatter:
        def __init__(self, i):
            self.prod, self.sib = prod.at[i], prod_sib.at[i]
            self.rin, self.rout = ring_in.at[i], ring_out.at[i]
            self.yout, self.yin = y_out.at[i], y_in.at[i]
            self.xout, self.xin = rows_out.at[i], rows_in.at[i]
            self.sibs, self.ring, self.seen = {}, {}, set()

        def give(self, b, left, right, dims):
            for n in range(0, WIDE, 512):
                if dims == 1:
                    term = dot(left, right[n:n + 512, :], ((1,), (1,)))
                else:
                    term = dot(left, right[:, n:n + 512])
                term = term.astype(BF16).reshape(4, 2, CHUNK, 512)
                for core in (0, 1):
                    self.prod[core, 4 * b:4 * b + 4, :, n:n + 512] = term[:, core]
            rows = pl.ds(4 * b, 4)
            self.sibs[b] = send(self.prod.at[1, rows], self.sib.at[rows], to_sib)

        def term(self, s, h):
            if s // 2 not in self.seen:
                self.seen.add(s // 2)
                self.sibs[s // 2].wait_recv()
            q = 2 * s + h
            return self.prod[0, q].astype(F32) + self.sib[q].astype(F32)

        def hop(self, way, dist, h):
            value = self.term(slot(way, dist), h)
            if (way, dist, h) in self.ring:
                self.ring[way, dist, h].wait_recv()
                value = value + self.rin[way, dist, h].astype(F32)
            self.rout[way, dist - 1, h] = value.astype(BF16)
            self.ring[way, dist - 1, h] = send(
                self.rout.at[way, dist - 1, h], self.rin.at[way, dist - 1, h], to_z[1 - way])

        def near(self, h):
            value = self.term(0, h)
            for way in (0, 1):
                self.ring[way, 0, h].wait_recv()
                value = value + self.rin[way, 0, h].astype(F32)
            return value

        def cross(self):
            self.yout[...] = self.near(1).astype(BF16)
            self.y = send(self.yout, self.yin, to_yh)

        def rows(self):
            value = self.near(0)
            self.y.wait_recv()
            value = value + self.yin[...].astype(F32)
            self.xout[...] = value.reshape(NX, ROWS, WIDE)
            self.x = [send(self.xout.at[xs[k]], self.xin.at[x], to_x[k]) for k in range(1, NX)]
            self.xin[x] = self.xout[x]

        def done(self):
            for copy in self.x:
                copy.wait_recv()
            return [self.xin[a] for a in range(NX)]

    class Weights:
        def __init__(self, i):
            self.sum, self.out, self.came = gsum.at[i], gsend.at[i], gin_got.at[i]

        def give(self, left_t, right):
            left = left_t[...]
            for n in range(4):
                cols = slice(n * UNITS, (n + 1) * UNITS)
                term = dot(left, right[:, :, cols].reshape(4 * BLOCK, UNITS))
                self.sum[n // 2, :, (n % 2) * UNITS:(n % 2 + 1) * UNITS] = term
            self.out[...] = self.sum[1 - yl].astype(BF16)
            self.copy = send(self.out, self.came, to_yl)

        def total(self):
            self.copy.wait_recv()
            return self.sum[yl] + self.came[...].astype(F32)

    ga, gg = Gather(acts), Gather(cots)
    fwd, bwd = Across(0, hid), Across(1, dpre)
    out, back = Scatter(0), Scatter(1)
    w_out, w_in = Weights(0), Weights(1)

    def pre(b):
        fwd.give(b, dot(ga.block(b), wi[...]))

    def act(b):
        value = fwd.total(b)
        cdf = 0.5 * (1.0 + lax.erf(value * 0.7071067811865476))
        slope[b] = cdf + value * jnp.exp(-0.5 * value * value) * 0.3989422804014327
        fwd.share(b, value * cdf)

    def cot(b):
        bwd.give(b, dot(gg.block(b), wo[...], ((1,), (1,))))

    def act_back(b):
        bwd.share(b, bwd.total(b) * slope[b])

    def branch(b):
        value = fwd.whole(b)
        hid_t[:, b * BLOCK:(b + 1) * BLOCK] = value.T
        out.give(b, value, wo, 0)

    def back_prod(b):
        value = bwd.whole(b)
        dpre_t[:, b * BLOCK:(b + 1) * BLOCK] = value.T
        back.give(b, value, wi, 1)

    ga.start()
    ga.other()
    ga.step(1)
    load_wi.wait()
    load_wo.wait()
    pre(0)
    ga.step(2)
    pre(1)
    act(0)
    ga.step(3)
    gg.start()
    pre(2)
    act(1)
    ga.step(4)
    gg.other()
    pre(3)
    act(2)
    gg.step(1)
    act(3)
    cot(0)
    branch(0)
    gg.step(2)
    cot(1)
    act_back(0)
    branch(1)
    branch(2)
    gg.step(3)
    branch(3)
    out.hop(0, 4, 0)
    out.hop(1, 4, 1)
    out.hop(0, 3, 1)
    out.hop(1, 3, 0)
    cot(2)
    act_back(1)
    gg.step(4)
    cot(3)
    act_back(2)
    out.hop(0, 3, 0)
    out.hop(1, 3, 1)
    back_prod(0)
    out.hop(0, 2, 1)
    out.hop(1, 2, 0)
    act_back(3)
    back_prod(1)
    out.hop(0, 2, 0)
    out.hop(1, 2, 1)
    back_prod(2)
    out.hop(0, 1, 1)
    out.hop(1, 1, 0)
    back_prod(3)
    out.hop(0, 1, 0)
    out.hop(1, 1, 1)
    back.hop(0, 4, 0)
    back.hop(1, 4, 1)
    back.hop(0, 3, 1)
    back.hop(1, 3, 0)
    out.cross()
    w_out.give(hid_t, cots)
    back.hop(0, 3, 0)
    back.hop(1, 3, 1)
    out.rows()
    back.hop(0, 2, 1)
    back.hop(1, 2, 0)
    w_in.give(dpre_t, acts)
    back.hop(0, 2, 0)
    back.hop(1, 2, 1)
    gres[...] = w_out.total()
    store_out = pltpu.make_async_copy(gres, gout_any, lsem.at[2])
    store_out.start()
    back.hop(0, 1, 1)
    back.hop(1, 1, 0)
    for a, piece in enumerate(out.done()):
        cols = slice(a * WIDE, (a + 1) * WIDE)
        mixed_ref[:, cols] = (x_ref[:, cols].astype(F32) + piece).astype(BF16)
    back.hop(0, 1, 0)
    back.hop(1, 1, 1)
    back.cross()
    grad_in_t = w_in.total()
    back.rows()
    gturn[...] = grad_in_t.T
    store_in = pltpu.make_async_copy(gturn, gin_any, lsem.at[3])
    store_in.start()

    scaled = [p * gain_ref[:, a * WIDE:(a + 1) * WIDE] for a, p in enumerate(back.done())]
    standards = [std[:, a * WIDE:(a + 1) * WIDE] for a in range(NX)]
    mean_scaled = sum(jnp.sum(s, axis=1, keepdims=True) for s in scaled) / x_ref.shape[1]
    mean_both = sum(
        jnp.sum(s * t, axis=1, keepdims=True) for s, t in zip(scaled, standards)) / x_ref.shape[1]
    for a in range(NX):
        cols = slice(a * WIDE, (a + 1) * WIDE)
        change = inv_scale * (scaled[a] - mean_scaled - standards[a] * mean_both)
        igrad_ref[:, cols] = (g_ref[:, cols].astype(F32) + change).astype(BF16)

    for copy in pending:
        copy.wait_send()
    store_out.wait()
    store_in.wait()


def local(block_in, norm_gain, weight_in, weight_out, output_grad):
    vmem, hbm = pl.BlockSpec(memory_space=pltpu.VMEM), pl.BlockSpec(memory_space=pl.ANY)
    rows, width = block_in.shape
    half = 2 * UNITS

    def buf(*shape, dtype=BF16):
        return pltpu.VMEM(shape, dtype)

    quarter = BLOCK // NX
    scratch = dict(
        wi=buf(WIDE, UNITS), wo=buf(UNITS, WIDE), std=buf(rows, width, dtype=F32),
        msg=buf(NX, 2 * ROWS, WIDE), got=buf(NX, 2 * ROWS, WIDE),
        acts=buf(32, CHUNK, WIDE), cots=buf(32, CHUNK, WIDE),
        part=buf(2, 4, NX, quarter, UNITS), part_in=buf(2, 4, NX - 1, quarter, UNITS),
        slope=buf(4, quarter, UNITS, dtype=F32),
        hid=buf(4, NX, quarter, UNITS), dpre=buf(4, NX, quarter, UNITS),
        hid_t=buf(UNITS, 4 * BLOCK), dpre_t=buf(UNITS, 4 * BLOCK),
        prod=buf(2, 2, 16, CHUNK, WIDE), prod_sib=buf(2, 16, CHUNK, WIDE),
        ring_in=buf(2, 2, 4, 2, CHUNK, WIDE), ring_out=buf(2, 2, 4, 2, CHUNK, WIDE),
        y_out=buf(2, CHUNK, WIDE), y_in=buf(2, CHUNK, WIDE),
        rows_out=buf(2, NX, ROWS, WIDE, dtype=F32), rows_in=buf(2, NX, ROWS, WIDE, dtype=F32),
        gsum=buf(2, 2, UNITS, half, dtype=F32), gsend=buf(2, UNITS, half),
        gin_got=buf(2, UNITS, half), gres=buf(UNITS, half, dtype=F32),
        gturn=buf(half, UNITS, dtype=F32),
        ssem=pltpu.SemaphoreType.DMA((SEMS,)), rsem=pltpu.SemaphoreType.DMA((SEMS,)),
        lsem=pltpu.SemaphoreType.DMA((4,)),
    )
    return pl.pallas_call(
        kernel,
        name="block",
        out_shape=(
            jax.ShapeDtypeStruct((rows, width), BF16),
            jax.ShapeDtypeStruct((rows, width), BF16),
            jax.ShapeDtypeStruct((half, UNITS), F32),
            jax.ShapeDtypeStruct((UNITS, half), F32),
        ),
        in_specs=[vmem, vmem, hbm, hbm, vmem],
        out_specs=(vmem, vmem, hbm, hbm),
        scratch_shapes=list(scratch.values()),
        compiler_params=pltpu.CompilerParams(
            collective_id=0, has_side_effects=True, vmem_limit_bytes=58 * 2**20
        ),
    )(block_in, norm_gain.reshape(1, width), weight_in, weight_out, output_grad)


def solution(mesh):
    in_specs = (P(("dp", "mp"), None), P(), P(None, "mp"), P("mp", None), P(("dp", "mp"), None))
    out_specs = (P(("dp", "mp"), None), P(("dp", "mp"), None), P("dp", "mp"), P("mp", "dp"))
    return jax.shard_map(local, mesh=mesh, in_specs=in_specs, out_specs=out_specs, check_vma=False)
```

time: 655 us -> 121 us (0.18)
  waiting for transfers between devices: 599 us -> 0 us
  Pallas kernels: 0 us -> 113 us
  matrix products: 29.4 us -> 0 us
  between operations: 14.2 us -> 0.64 us
  other arithmetic: 11 us -> 0 us
    reduce_scatter x4 -> x0, waiting for transfers between devices: 434 us -> none  [the longest x1 125 us: local(): lax.psum_scatter(jnp.dot(block, weight_out, preferred_element_type=jnp.fl...]
    all_gather x2 -> x0, waiting for transfers between devices: 165 us -> none  [the longest x1 86.9 us: local(): normed_all = lax.all_gather(normed, 'mp', axis=0, tiled=True)]
    pallas_call x0 -> x1, Pallas kernels: none -> 113 us  [local(): pl.pallas_call(kernel, name='block', out_shape=(jax.ShapeDtypeStruct((row...]
    dot_general x6 -> x0, matrix products: 29.4 us -> none  [the longest x2 9.8 us: contract_rows(): lax.dot_general(left, right, (((0,), (0,)), ((), ())), preferred_element_...]
    convert_element_type x4 -> x0, other arithmetic: 7.66 us -> none  [the longest x2 4.31 us: local(): grad_in, grad_out = (lax.psum_scatter(term_in.astype(jnp.bfloat16), 'dp',...]
  transfers between devices with their start and end apart: 6 -> 0, of which waited for: 6 -> 0; matrix products, arithmetic and copies ran while one was open for 4% -> 0% of each run, Pallas kernels for 0% -> 0%
where the time goes in v1:
time: 121 us
  Pallas kernels  113 us (93%)
  local copies, waits for them, and re-layouts  6.55 us (5%)
    pallas_call x1, Pallas kernels, local(): pl.pallas_call(kernel, name='block', out_shape=(jax.ShapeDtypeStruct((row...  113 us
    unnamed x6, local copies, waits for them, and re-layouts  6.55 us

profile of v1, /device:TPU:1, one launch (start us, length us, event | category | flops | bytes accessed | tf_op | source)
XLA Modules:
  0.0 120.6 jit_solution(17293819248396331550)
XLA Ops:
  0.6 113.4 %block.1 = (bf16[8,6144]{1,0:T(8,128)(2,1)}, bf16[8,6144]{1,0:T(8,128)(2,1)}, f32[768,384]{1,0:T(8,128)}, f32[384,768]{1,0:T(8,128)}) custom-call(bf16[8,6144]{1,0:T(8,128)(2,1)} %x_ref.1, f32[1,6144]{1,0:T(1,128)} %bitcast.1, bf16[6144,384]{1,0:T(8,128)(2,1)} %wi_any.1, bf16[384,6144]{1,0:T(8,128)(2,1)} %wo_any.1, bf16[8,6144]{1,0:T(8,128)(2,1)} %g_ref.1), custom_call_target="tpu_custom_call" | custom-call | tf_op jit(solution)/shard_map/block/pallas_call | solution.py:408
  114.0 1.5 %copy.13 = bf16[8,6144]{1,0:T(8,128)(2,1)} copy(bf16[8,6144]{1,0:T(8,128)(2,1)} %get-tuple-element.8) | data formatting | bytes 196608
  115.6 1.5 %copy.14 = bf16[8,6144]{1,0:T(8,128)(2,1)} copy(bf16[8,6144]{1,0:T(8,128)(2,1)} %get-tuple-element.9) | data formatting | bytes 196608
  117.1 0.0 copy-start
  117.1 2.5 %copy.15 = f32[768,384]{1,0:T(8,128)} copy(f32[768,384]{1,0:T(8,128)} %get-tuple-element.10) | data formatting | bytes 2359296
  119.5 0.0 copy-done
  119.6 1.0 copy.16
Async XLA Ops:
  117.1 2.5 %copy-start = (f32[384,768]{1,0:T(8,128)S(1)}, f32[384,768]{1,0:T(8,128)}, u32[]{:S(2)}) copy-start(f32[384,768]{1,0:T(8,128)} %get-tuple-element.11) | copy-start | bytes 3538948

commit v2 on v1

v2 whole, which is shorter than its diff:
```python
import jax
import jax.numpy as jnp
from jax import lax
from jax.experimental import pallas as pl
from jax.experimental.pallas import tpu as pltpu
from jax.sharding import PartitionSpec as P

MESH = pl.DeviceIdType.MESH
F32, BF16 = jnp.float32, jnp.bfloat16

NX, NZ = 4, 8
ROWS = 8
CHUNK = NX * ROWS
WIDE = 1536
UNITS = 384
BLOCK = 256
HALF = CHUNK // 2
PER = BLOCK // (4 * HALF)
FAR = 3
SEMS = 320


def place():
    dp, mp = lax.axis_index("dp"), lax.axis_index("mp")
    return (
        lax.div(dp, 2),
        lax.rem(dp, 2),
        lax.div(mp, 16),
        lax.rem(lax.div(mp, 2), NZ),
        lax.rem(mp, 2),
    )


def device(x, yl, yh, z, c):
    return (x * 2 + yl, (yh * NZ + z) * 2 + c)


def slot(way, dist):
    if dist == 0:
        return 0
    if dist == 4:
        return 7
    return 2 * dist - 1 + way


def dot(left, right, dims=((1,), (0,))):
    return lax.dot_general(left, right, (dims, ((), ())), preferred_element_type=F32)


def kernel(
    x_ref, gain_ref, wi_any, wo_any, g_ref,
    mixed_ref, igrad_ref, gin_any, gout_any,
    wi, wo, std, msg, got, acts, cots,
    terms, terms_in, slope, hid, dpre, hid_t, dpre_t,
    prod, prod_sib, ring_in, ring_out, y_out, y_in, rows_out, rows_in,
    gsum, gsend, gin_got, gres, gturn,
    ssem, rsem, lsem,
):
    x, yl, yh, z, c = place()
    xs = [lax.rem(x + k, NX) for k in range(NX)]
    zp, zm = lax.rem(z + 1, NZ), lax.rem(z + NZ - 1, NZ)
    to_z = (device(x, yl, yh, zp, c), device(x, yl, yh, zm, c))
    to_sib = device(x, yl, yh, z, 1 - c)
    to_yh = device(x, yl, 1 - yh, z, c)
    to_yl = device(x, 1 - yl, yh, z, c)
    to_x = [device(xs[k], yl, yh, z, c) for k in range(NX)]

    barrier = pltpu.get_barrier_semaphore()
    for other in (*to_z, to_sib, to_yh, to_yl, *to_x[1:]):
        pl.semaphore_signal(barrier, inc=1, device_id=other, device_id_type=MESH)

    load_wi = pltpu.make_async_copy(
        wi_any.at[pl.ds(pl.multiple_of(x * WIDE, WIDE), WIDE)], wi, lsem.at[0])
    load_wo = pltpu.make_async_copy(
        wo_any.at[:, pl.ds(pl.multiple_of(x * WIDE, WIDE), WIDE)], wo, lsem.at[1])
    load_wi.start()
    load_wo.start()

    values = x_ref[...].astype(F32)
    average = jnp.mean(values, axis=1, keepdims=True)
    centred = values - average
    inv_scale = lax.rsqrt(jnp.mean(centred * centred, axis=1, keepdims=True) + 1e-06)
    standard = centred * inv_scale
    std[...] = standard
    normed = standard * gain_ref[...]
    grad = g_ref[...].astype(F32)
    for q in range(NX):
        cols = slice(q * WIDE, (q + 1) * WIDE)
        msg[q] = jnp.concatenate([normed[:, cols], grad[:, cols]], axis=0).astype(BF16)

    pl.semaphore_wait(barrier, 8)

    pending = []

    def send(src, dst, to):
        k = len(pending)
        copy = pltpu.make_async_remote_copy(
            src_ref=src, dst_ref=dst, send_sem=ssem.at[k], recv_sem=rsem.at[k],
            device_id=to, device_id_type=MESH)
        copy.start()
        pending.append(copy)
        return copy

    first = [send(msg.at[xs[k]], got.at[x], to_x[k]) for k in range(1, NX)]
    got[x] = msg[x]
    for copy in first:
        copy.wait_recv()
    pieces = [got[a].astype(F32) for a in range(NX)]
    for part in (0, 1):
        pair = pieces[2 * part:2 * part + 2]
        acts[part, 0] = jnp.concatenate([p[:ROWS] for p in pair], axis=0).astype(BF16)
        cots[part, 0] = jnp.concatenate([p[ROWS:] for p in pair], axis=0).astype(BF16)

    def ways(dist, part, turn):
        return (0, 1) if dist < 4 else (part ^ turn,)

    class Gather:
        def __init__(self, buf, turn):
            self.buf, self.turn = buf, turn
            self.near, self.ring, self.y, self.sib = {}, {}, {}, {}

        def at(self, part, s, h):
            return self.buf.at[part, 4 * s + h]

        def pass_on(self, part, way, dist, h):
            here = self.at(part, slot(way, dist), h)
            if dist < (FAR - 1 if h else 4) and way in ways(dist + 1, part, self.turn):
                there = self.at(part, slot(way, dist + 1), h)
                self.ring[part, way, dist + 1, h] = send(here, there, to_z[way])
            if dist >= FAR and h == 0:
                there = self.at(part, slot(way, dist), 1)
                self.y[part, way, dist] = send(here, there, to_yh)

        def to_core(self, part, s):
            self.sib[part, s] = send(
                self.buf.at[part, pl.ds(4 * s, 2)], self.buf.at[part, pl.ds(4 * s + 2, 2)], to_sib)

        def start(self, part):
            self.near[part] = send(self.at(part, 0, 0), self.at(part, 0, 1), to_yh)
            for way in (0, 1):
                self.pass_on(part, way, 0, 0)

        def other(self, part):
            self.near[part].wait_recv()
            for way in (0, 1):
                self.pass_on(part, way, 0, 1)
            self.to_core(part, 0)

        def own(self, part, dist):
            for way in ways(dist, part, self.turn):
                self.ring[part, way, dist, 0].wait_recv()
                self.pass_on(part, way, dist, 0)

        def oth(self, part, dist):
            for way in (0, 1):
                self.ring[part, way, dist, 1].wait_recv()
                self.pass_on(part, way, dist, 1)
                self.to_core(part, slot(way, dist))

        def far(self, part, dist):
            for way in ways(dist, part, self.turn):
                self.y[part, way, dist].wait_recv()
                self.to_core(part, slot(way, dist))

        def block(self, part, b):
            for s in range(PER * b, PER * b + PER):
                self.sib[part, s].wait_recv()
            return self.buf[part, 4 * PER * b:4 * PER * (b + 1)].reshape(BLOCK, WIDE)

    class Across:
        def __init__(self, i, result):
            self.term, self.came, self.result = terms.at[i], terms_in.at[i], result
            self.out, self.back = {}, {}

        def give(self, b, term):
            self.term[b] = term.astype(BF16).reshape(NX, BLOCK // NX, UNITS)
            self.out[b] = [
                send(self.term.at[b, xs[k]], self.came.at[b, k - 1], to_x[k]) for k in range(1, NX)]

        def total(self, b):
            for copy in self.out[b]:
                copy.wait_recv()
            total = self.term[b, x].astype(F32)
            for k in range(NX - 1):
                total = total + self.came[b, k].astype(F32)
            return total

        def share(self, b, value):
            self.result[b, x] = value.astype(BF16)
            self.back[b] = [
                send(self.result.at[b, x], self.result.at[b, x], to_x[k]) for k in range(1, NX)]

        def whole(self, b):
            for copy in self.back[b]:
                copy.wait_recv()
            return self.result[b].reshape(BLOCK, UNITS)

    class Scatter:
        def __init__(self, i, turn):
            self.turn = turn
            self.prod, self.sib = prod.at[i], prod_sib.at[i]
            self.rin, self.rout = ring_in.at[i], ring_out.at[i]
            self.yout, self.yin = y_out.at[i], y_in.at[i]
            self.xout, self.xin = rows_out.at[i], rows_in.at[i]
            self.sibs, self.ring, self.y, self.seen = {}, {}, {}, set()

        def give(self, k, left, right, dims):
            for n in range(0, WIDE, 512):
                if dims == 1:
                    term = dot(left, right[n:n + 512, :], ((1,), (1,)))
                else:
                    term = dot(left, right[:, n:n + 512])
                term = term.astype(BF16).reshape(PER, 2, 2, HALF, 512)
                for core in (0, 1):
                    self.prod[core, k, :, :, n:n + 512] = term[:, core].reshape(2 * PER, HALF, 512)
            self.sibs[k] = send(self.prod.at[1, k], self.sib.at[k], to_sib)

        def term(self, part, s, h):
            k, q = 2 * part + s // PER, 2 * (s % PER) + h
            if k not in self.seen:
                self.seen.add(k)
                self.sibs[k].wait_recv()
            return self.prod[0, k, q].astype(F32) + self.sib[k, q].astype(F32)

        def hop(self, part, way, dist, h):
            value = self.term(part, slot(way, dist), h)
            if (part, way, dist, h) in self.ring:
                self.ring[part, way, dist, h].wait_recv()
                value = value + self.rin[part, way, dist, h].astype(F32)
            self.rout[part, way, dist - 1, h] = value.astype(BF16)
            self.ring[part, way, dist - 1, h] = send(
                self.rout.at[part, way, dist - 1, h], self.rin.at[part, way, dist - 1, h],
                to_z[1 - way])

        def hops(self, part, dist, h):
            for way in ways(dist, part, self.turn):
                self.hop(part, way, dist, h)

        def near(self, part, h):
            value = self.term(part, 0, h)
            for way in (0, 1):
                self.ring[part, way, 0, h].wait_recv()
                value = value + self.rin[part, way, 0, h].astype(F32)
            return value

        def cross(self, part):
            self.yout[part] = self.near(part, 1).astype(BF16)
            self.y[part] = send(self.yout.at[part], self.yin.at[part], to_yh)

        def rows(self, part):
            value = self.near(part, 0)
            self.y[part].wait_recv()
            value = value + self.yin[part].astype(F32)
            self.xout[2 * part:2 * part + 2] = value.reshape(2, ROWS, WIDE)

        def across(self):
            self.x = [send(self.xout.at[xs[k]], self.xin.at[x], to_x[k]) for k in range(1, NX)]
            self.xin[x] = self.xout[x]

        def done(self):
            for copy in self.x:
                copy.wait_recv()
            return [self.xin[a] for a in range(NX)]

    class Weights:
        def __init__(self, i):
            self.sum, self.out, self.came = gsum.at[i], gsend.at[i], gin_got.at[i]

        def give(self, left_t, right):
            left = left_t[...]
            for n in range(4):
                cols = slice(n * UNITS, (n + 1) * UNITS)
                term = dot(left, right[:, :, :, cols].reshape(4 * BLOCK, UNITS))
                self.sum[n // 2, :, (n % 2) * UNITS:(n % 2 + 1) * UNITS] = term
            self.out[...] = self.sum[1 - yl].astype(BF16)
            self.copy = send(self.out, self.came, to_yl)

        def total(self):
            self.copy.wait_recv()
            return self.sum[yl] + self.came[...].astype(F32)

    ga, gg = Gather(acts, 0), Gather(cots, 1)
    fwd, bwd = Across(0, hid), Across(1, dpre)
    out, back = Scatter(0, 0), Scatter(1, 1)
    w_out, w_in = Weights(0), Weights(1)

    def pre(part, b):
        fwd.give(2 * part + b, dot(ga.block(part, b), wi[...]))

    def act(part, b):
        k = 2 * part + b
        value = fwd.total(k)
        cdf = 0.5 * (1.0 + lax.erf(value * 0.7071067811865476))
        slope[k] = cdf + value * jnp.exp(-0.5 * value * value) * 0.3989422804014327
        fwd.share(k, value * cdf)

    def cot(part, b):
        bwd.give(2 * part + b, dot(gg.block(part, b), wo[...], ((1,), (1,))))

    def act_back(part, b):
        k = 2 * part + b
        bwd.share(k, bwd.total(k) * slope[k])

    def branch(part, b):
        k = 2 * part + b
        value = fwd.whole(k)
        hid_t[:, k * BLOCK:(k + 1) * BLOCK] = value.T
        out.give(k, value, wo, 0)

    def back_prod(part, b):
        k = 2 * part + b
        value = bwd.whole(k)
        dpre_t[:, k * BLOCK:(k + 1) * BLOCK] = value.T
        back.give(k, value, wi, 1)

    def mixed():
        for a, piece in enumerate(out.done()):
            cols = slice(a * WIDE, (a + 1) * WIDE)
            mixed_ref[:, cols] = (x_ref[:, cols].astype(F32) + piece).astype(BF16)

    def store_out_grad():
        gres[...] = w_out.total()
        store_out.start()

    def store_in_grad():
        gturn[...] = w_in.total().T
        store_in.start()

    def finish():
        scaled = [p * gain_ref[:, a * WIDE:(a + 1) * WIDE] for a, p in enumerate(back.done())]
        standards = [std[:, a * WIDE:(a + 1) * WIDE] for a in range(NX)]
        mean_scaled = sum(jnp.sum(s, axis=1, keepdims=True) for s in scaled) / x_ref.shape[1]
        mean_both = sum(
            jnp.sum(s * t, axis=1, keepdims=True)
            for s, t in zip(scaled, standards)) / x_ref.shape[1]
        for a in range(NX):
            cols = slice(a * WIDE, (a + 1) * WIDE)
            change = inv_scale * (scaled[a] - mean_scaled - standards[a] * mean_both)
            igrad_ref[:, cols] = (g_ref[:, cols].astype(F32) + change).astype(BF16)

    store_out = pltpu.make_async_copy(gres, gout_any, lsem.at[2])
    store_in = pltpu.make_async_copy(gturn, gin_any, lsem.at[3])

    ga.start(0)
    ga.start(1)
    ga.own(0, 1)
    ga.other(0)
    ga.own(1, 1)
    ga.other(1)
    ga.own(0, 2)
    ga.oth(0, 1)
    gg.start(0)
    ga.own(1, 2)
    gg.start(1)
    ga.oth(1, 1)
    ga.own(0, 3)
    ga.oth(0, 2)
    load_wi.wait()
    load_wo.wait()
    pre(0, 0)
    gg.other(0)
    gg.own(0, 1)
    ga.own(1, 3)
    gg.other(1)
    gg.own(1, 1)
    ga.far(0, 3)
    ga.oth(1, 2)
    ga.own(0, 4)
    gg.oth(0, 1)
    act(0, 0)
    ga.far(1, 3)
    gg.own(0, 2)
    pre(1, 0)
    ga.own(1, 4)
    gg.oth(1, 1)
    ga.far(0, 4)
    gg.own(1, 2)
    pre(0, 1)
    branch(0, 0)
    ga.far(1, 4)
    act(1, 0)
    gg.own(0, 3)
    gg.oth(1, 2)
    gg.own(1, 3)
    pre(1, 1)
    cot(1, 0)
    gg.own(0, 4)
    gg.own(1, 4)
    branch(1, 0)
    gg.far(0, 3)
    act(0, 1)
    gg.oth(0, 2)
    act(1, 1)
    gg.far(1, 3)
    cot(0, 0)
    act_back(1, 0)
    gg.far(1, 4)
    gg.far(0, 4)
    branch(0, 1)
    cot(0, 1)
    cot(1, 1)
    branch(1, 1)
    w_out.give(hid_t, cots)
    out.hops(1, 4, 1)
    out.hops(1, 4, 0)
    out.hops(0, 4, 0)
    out.hops(0, 4, 1)
    act_back(0, 0)
    back_prod(1, 0)
    act_back(0, 1)
    out.hops(0, 3, 0)
    act_back(1, 1)
    out.hops(0, 3, 1)
    out.hops(1, 3, 1)
    out.hops(1, 3, 0)
    back_prod(0, 0)
    out.hops(0, 2, 0)
    back_prod(0, 1)
    out.hops(0, 2, 1)
    out.hops(1, 2, 1)
    back_prod(1, 1)
    back.hops(0, 4, 1)
    back.hops(0, 4, 0)
    out.hops(0, 1, 0)
    out.hops(0, 1, 1)
    back.hops(1, 4, 1)
    out.hops(1, 2, 0)
    out.hops(1, 1, 1)
    back.hops(1, 4, 0)
    w_in.give(dpre_t, acts)
    back.hops(0, 3, 0)
    back.hops(0, 3, 1)
    store_out_grad()
    back.hops(1, 3, 1)
    back.hops(1, 3, 0)
    out.hops(1, 1, 0)
    back.hops(0, 2, 1)
    back.hops(1, 2, 1)
    back.hops(1, 2, 0)
    out.cross(0)
    out.cross(1)
    back.hops(0, 2, 0)
    back.hops(0, 1, 1)
    back.hops(1, 1, 1)
    back.hops(1, 1, 0)
    back.hops(0, 1, 0)
    back.cross(0)
    back.cross(1)
    store_in_grad()
    out.rows(0)
    out.rows(1)
    out.across()
    back.rows(0)
    back.rows(1)
    back.across()
    mixed()
    finish()

    for copy in pending:
        copy.wait_send()
    store_out.wait()
    store_in.wait()


def local(block_in, norm_gain, weight_in, weight_out, output_grad):
    vmem, hbm = pl.BlockSpec(memory_space=pltpu.VMEM), pl.BlockSpec(memory_space=pl.ANY)
    rows, width = block_in.shape
    half = 2 * UNITS

    def buf(*shape, dtype=BF16):
        return pltpu.VMEM(shape, dtype)

    quarter = BLOCK // NX
    scratch = dict(
        wi=buf(WIDE, UNITS), wo=buf(UNITS, WIDE), std=buf(rows, width, dtype=F32),
        msg=buf(NX, 2 * ROWS, WIDE), got=buf(NX, 2 * ROWS, WIDE),
        acts=buf(2, 32, HALF, WIDE), cots=buf(2, 32, HALF, WIDE),
        terms=buf(2, 4, NX, quarter, UNITS), terms_in=buf(2, 4, NX - 1, quarter, UNITS),
        slope=buf(4, quarter, UNITS, dtype=F32),
        hid=buf(4, NX, quarter, UNITS), dpre=buf(4, NX, quarter, UNITS),
        hid_t=buf(UNITS, 4 * BLOCK), dpre_t=buf(UNITS, 4 * BLOCK),
        prod=buf(2, 2, 4, 2 * PER, HALF, WIDE), prod_sib=buf(2, 4, 2 * PER, HALF, WIDE),
        ring_in=buf(2, 2, 2, 4, 2, HALF, WIDE), ring_out=buf(2, 2, 2, 4, 2, HALF, WIDE),
        y_out=buf(2, 2, HALF, WIDE), y_in=buf(2, 2, HALF, WIDE),
        rows_out=buf(2, NX, ROWS, WIDE, dtype=F32), rows_in=buf(2, NX, ROWS, WIDE, dtype=F32),
        gsum=buf(2, 2, UNITS, half, dtype=F32), gsend=buf(2, UNITS, half),
        gin_got=buf(2, UNITS, half), gres=buf(UNITS, half, dtype=F32),
        gturn=buf(half, UNITS, dtype=F32),
        ssem=pltpu.SemaphoreType.DMA((SEMS,)), rsem=pltpu.SemaphoreType.DMA((SEMS,)),
        lsem=pltpu.SemaphoreType.DMA((4,)),
    )
    return pl.pallas_call(
        kernel,
        name="block",
        out_shape=(
            jax.ShapeDtypeStruct((rows, width), BF16),
            jax.ShapeDtypeStruct((rows, width), BF16),
            jax.ShapeDtypeStruct((half, UNITS), F32),
            jax.ShapeDtypeStruct((UNITS, half), F32),
        ),
        in_specs=[vmem, vmem, hbm, hbm, vmem],
        out_specs=(vmem, vmem, hbm, hbm),
        scratch_shapes=list(scratch.values()),
        compiler_params=pltpu.CompilerParams(
            collective_id=0, has_side_effects=True, vmem_limit_bytes=58 * 2**20
        ),
    )(block_in, norm_gain.reshape(1, width), weight_in, weight_out, output_grad)


def solution(mesh):
    in_specs = (P(("dp", "mp"), None), P(), P(None, "mp"), P("mp", None), P(("dp", "mp"), None))
    out_specs = (P(("dp", "mp"), None), P(("dp", "mp"), None), P("dp", "mp"), P("mp", "dp"))
    return jax.shard_map(local, mesh=mesh, in_specs=in_specs, out_specs=out_specs, check_vma=False)
```

time: 121 us -> 112 us (0.926); the launches traced: 121 us -> 110 us
  Pallas kernels: 113 us -> 103 us
    pallas_call x1, Pallas kernels: 113 us -> 103 us  [local(): pl.pallas_call(kernel, name='block', out_shape=(jax.ShapeDtypeStruct((row...]
where the time goes in v2:
time: 112 us; the launch traced here: 110 us
  Pallas kernels  103 us (92%)
  local copies, waits for them, and re-layouts  6.55 us (6%)
    pallas_call x1, Pallas kernels, local(): pl.pallas_call(kernel, name='block', out_shape=(jax.ShapeDtypeStruct((row...  103 us
    unnamed x6, local copies, waits for them, and re-layouts  6.55 us

profile of v2, /device:TPU:1, one launch (start us, length us, event | category | flops | bytes accessed | tf_op | source)
XLA Modules:
  0.0 110.0 jit_solution(8332787124286949374)
XLA Ops:
  0.6 102.8 %block.1 = (bf16[8,6144]{1,0:T(8,128)(2,1)}, bf16[8,6144]{1,0:T(8,128)(2,1)}, f32[768,384]{1,0:T(8,128)}, f32[384,768]{1,0:T(8,128)}) custom-call(bf16[8,6144]{1,0:T(8,128)(2,1)} %x_ref.1, f32[1,6144]{1,0:T(1,128)} %bitcast.1, bf16[6144,384]{1,0:T(8,128)(2,1)} %wi_any.1, bf16[384,6144]{1,0:T(8,128)(2,1)} %wo_any.1, bf16[8,6144]{1,0:T(8,128)(2,1)} %g_ref.1), custom_call_target="tpu_custom_call" | custom-call | tf_op jit(solution)/shard_map/block/pallas_call | solution.py:492
  103.5 1.5 %copy.13 = bf16[8,6144]{1,0:T(8,128)(2,1)} copy(bf16[8,6144]{1,0:T(8,128)(2,1)} %get-tuple-element.8) | data formatting | bytes 196608
  105.0 1.5 %copy.14 = bf16[8,6144]{1,0:T(8,128)(2,1)} copy(bf16[8,6144]{1,0:T(8,128)(2,1)} %get-tuple-element.9) | data formatting | bytes 196608
  106.6 0.0 copy-start
  106.6 2.5 %copy.15 = f32[768,384]{1,0:T(8,128)} copy(f32[768,384]{1,0:T(8,128)} %get-tuple-element.10) | data formatting | bytes 2359296
  109.0 0.0 copy-done
  109.0 1.0 copy.16
Async XLA Ops:
  106.6 2.5 %copy-start = (f32[384,768]{1,0:T(8,128)S(1)}, f32[384,768]{1,0:T(8,128)}, u32[]{:S(2)}) copy-start(f32[384,768]{1,0:T(8,128)} %get-tuple-element.11) | copy-start | bytes 3538948

commit v3 on v2

--- a/solution.py
+++ b/solution.py
@@ -18,6 +18,7 @@
 PER = BLOCK // (4 * HALF)
 FAR = 3
 SEMS = 320
+VMEM_ASKED = 60 * 2**20
 
 
 def place():
@@ -47,13 +48,62 @@
     return lax.dot_general(left, right, (dims, ((), ())), preferred_element_type=F32)
 
 
+def standardise(x_ref):
+    values = x_ref[...].astype(F32)
+    average = jnp.mean(values, axis=1, keepdims=True)
+    centred = values - average
+    inv_scale = lax.rsqrt(jnp.mean(centred * centred, axis=1, keepdims=True) + 1e-06)
+    return centred * inv_scale, inv_scale
+
+
+def finish_kernel(
+    x_any, gain_any, g_any, rows_any, gin_any, gout_any,
+    mixed_any, igrad_any, gin_out, gout_out,
+    x_ref, gain_ref, g_ref, rows, gin, turned, gout, mixed, igrad, sems, osems,
+):
+    pairs = (
+        (gin_any, gin), (x_any, x_ref), (gain_any, gain_ref), (g_any, g_ref), (rows_any, rows),
+        (gout_any, gout))
+    loads = [pltpu.make_async_copy(a, b, sems.at[k]) for k, (a, b) in enumerate(pairs)]
+    for copy in loads:
+        copy.start()
+    stores = [
+        pltpu.make_async_copy(a, b, osems.at[k])
+        for k, (a, b) in enumerate((
+            (turned, gin_out), (mixed, mixed_any), (igrad, igrad_any), (gout, gout_out)))]
+    loads[0].wait()
+    turned[...] = gin[...].T
+    stores[0].start()
+    for copy in loads[1:]:
+        copy.wait()
+    stores[3].start()
+    width = x_ref.shape[1]
+    for a in range(NX):
+        cols = slice(a * WIDE, (a + 1) * WIDE)
+        mixed[:, cols] = (x_ref[:, cols].astype(F32) + rows[0, a]).astype(BF16)
+    stores[1].start()
+    standard, inv_scale = standardise(x_ref)
+    scaled = [rows[1, a] * gain_ref[:, a * WIDE:(a + 1) * WIDE] for a in range(NX)]
+    standards = [standard[:, a * WIDE:(a + 1) * WIDE] for a in range(NX)]
+    mean_scaled = sum(jnp.sum(s, axis=1, keepdims=True) for s in scaled) / width
+    mean_both = sum(
+        jnp.sum(s * t, axis=1, keepdims=True) for s, t in zip(scaled, standards)) / width
+    for a in range(NX):
+        cols = slice(a * WIDE, (a + 1) * WIDE)
+        change = inv_scale * (scaled[a] - mean_scaled - standards[a] * mean_both)
+        igrad[:, cols] = (g_ref[:, cols].astype(F32) + change).astype(BF16)
+    stores[2].start()
+    for copy in stores:
+        copy.wait()
+
+
 def kernel(
-    x_ref, gain_ref, wi_any, wo_any, g_ref,
-    mixed_ref, igrad_ref, gin_any, gout_any,
-    wi, wo, std, msg, got, acts, cots,
+    x_any, gain_any, wi_any, wo_any, g_any,
+    rows_any, gin_any, gout_any,
+    x_ref, gain_ref, g_ref, wi, wo, msg, got, acts, cots,
     terms, terms_in, slope, hid, dpre, hid_t, dpre_t,
     prod, prod_sib, ring_in, ring_out, y_out, y_in, rows_out, rows_in,
-    gsum, gsend, gin_got, gres, gturn,
+    gsum, gsend, gin_got, gres,
     ssem, rsem, lsem,
 ):
     x, yl, yh, z, c = place()
@@ -73,16 +123,17 @@
         wi_any.at[pl.ds(pl.multiple_of(x * WIDE, WIDE), WIDE)], wi, lsem.at[0])
     load_wo = pltpu.make_async_copy(
         wo_any.at[:, pl.ds(pl.multiple_of(x * WIDE, WIDE), WIDE)], wo, lsem.at[1])
+    loads = [
+        pltpu.make_async_copy(src, dst, lsem.at[4 + k])
+        for k, (src, dst) in enumerate(((x_any, x_ref), (gain_any, gain_ref), (g_any, g_ref)))]
+    for copy in loads:
+        copy.start()
     load_wi.start()
     load_wo.start()
-
-    values = x_ref[...].astype(F32)
-    average = jnp.mean(values, axis=1, keepdims=True)
-    centred = values - average
-    inv_scale = lax.rsqrt(jnp.mean(centred * centred, axis=1, keepdims=True) + 1e-06)
-    standard = centred * inv_scale
-    std[...] = standard
-    normed = standard * gain_ref[...]
+    for copy in loads:
+        copy.wait()
+
+    normed = standardise(x_ref)[0] * gain_ref[...]
     grad = g_ref[...].astype(F32)
     for q in range(NX):
         cols = slice(q * WIDE, (q + 1) * WIDE)
@@ -260,7 +311,6 @@
         def done(self):
             for copy in self.x:
                 copy.wait_recv()
-            return [self.xin[a] for a in range(NX)]
 
     class Weights:
         def __init__(self, i):
@@ -314,32 +364,25 @@
         back.give(k, value, wi, 1)
 
     def mixed():
-        for a, piece in enumerate(out.done()):
-            cols = slice(a * WIDE, (a + 1) * WIDE)
-            mixed_ref[:, cols] = (x_ref[:, cols].astype(F32) + piece).astype(BF16)
+        out.done()
+        keep_out.start()
 
     def store_out_grad():
-        gres[...] = w_out.total()
+        gres[0] = w_out.total()
         store_out.start()
 
     def store_in_grad():
-        gturn[...] = w_in.total().T
+        gres[1] = w_in.total()
         store_in.start()
 
     def finish():
-        scaled = [p * gain_ref[:, a * WIDE:(a + 1) * WIDE] for a, p in enumerate(back.done())]
-        standards = [std[:, a * WIDE:(a + 1) * WIDE] for a in range(NX)]
-        mean_scaled = sum(jnp.sum(s, axis=1, keepdims=True) for s in scaled) / x_ref.shape[1]
-        mean_both = sum(
-            jnp.sum(s * t, axis=1, keepdims=True)
-            for s, t in zip(scaled, standards)) / x_ref.shape[1]
-        for a in range(NX):
-            cols = slice(a * WIDE, (a + 1) * WIDE)
-            change = inv_scale * (scaled[a] - mean_scaled - standards[a] * mean_both)
-            igrad_ref[:, cols] = (g_ref[:, cols].astype(F32) + change).astype(BF16)
-
-    store_out = pltpu.make_async_copy(gres, gout_any, lsem.at[2])
-    store_in = pltpu.make_async_copy(gturn, gin_any, lsem.at[3])
+        back.done()
+        keep_back.start()
+
+    store_out = pltpu.make_async_copy(gres.at[0], gout_any, lsem.at[2])
+    store_in = pltpu.make_async_copy(gres.at[1], gin_any, lsem.at[3])
+    keep_out = pltpu.make_async_copy(rows_in.at[0], rows_any.at[0], lsem.at[7])
+    keep_back = pltpu.make_async_copy(rows_in.at[1], rows_any.at[1], lsem.at[8])
 
     ga.start(0)
     ga.start(1)
@@ -458,21 +501,23 @@
 
     for copy in pending:
         copy.wait_send()
-    store_out.wait()
-    store_in.wait()
+    for copy in (store_out, store_in, keep_out, keep_back):
+        copy.wait()
 
 
 def local(block_in, norm_gain, weight_in, weight_out, output_grad):
-    vmem, hbm = pl.BlockSpec(memory_space=pltpu.VMEM), pl.BlockSpec(memory_space=pl.ANY)
+    hbm = pl.BlockSpec(memory_space=pl.ANY)
     rows, width = block_in.shape
     half = 2 * UNITS
+    gain = norm_gain.reshape(1, width)
 
     def buf(*shape, dtype=BF16):
         return pltpu.VMEM(shape, dtype)
 
     quarter = BLOCK // NX
+    inputs = dict(x=buf(rows, width), gain=buf(1, width, dtype=F32), g=buf(rows, width))
     scratch = dict(
-        wi=buf(WIDE, UNITS), wo=buf(UNITS, WIDE), std=buf(rows, width, dtype=F32),
+        **inputs, wi=buf(WIDE, UNITS), wo=buf(UNITS, WIDE),
         msg=buf(NX, 2 * ROWS, WIDE), got=buf(NX, 2 * ROWS, WIDE),
         acts=buf(2, 32, HALF, WIDE), cots=buf(2, 32, HALF, WIDE),
         terms=buf(2, 4, NX, quarter, UNITS), terms_in=buf(2, 4, NX - 1, quarter, UNITS),
@@ -484,27 +529,43 @@
         y_out=buf(2, 2, HALF, WIDE), y_in=buf(2, 2, HALF, WIDE),
         rows_out=buf(2, NX, ROWS, WIDE, dtype=F32), rows_in=buf(2, NX, ROWS, WIDE, dtype=F32),
         gsum=buf(2, 2, UNITS, half, dtype=F32), gsend=buf(2, UNITS, half),
-        gin_got=buf(2, UNITS, half), gres=buf(UNITS, half, dtype=F32),
-        gturn=buf(half, UNITS, dtype=F32),
+        gin_got=buf(2, UNITS, half), gres=buf(2, UNITS, half, dtype=F32),
         ssem=pltpu.SemaphoreType.DMA((SEMS,)), rsem=pltpu.SemaphoreType.DMA((SEMS,)),
-        lsem=pltpu.SemaphoreType.DMA((4,)),
+        lsem=pltpu.SemaphoreType.DMA((9,)),
     )
-    return pl.pallas_call(
+    summed, gin_t, gout = pl.pallas_call(
         kernel,
         name="block",
+        out_shape=(
+            jax.ShapeDtypeStruct((2, NX, rows, WIDE), F32),
+            jax.ShapeDtypeStruct((UNITS, half), F32),
+            jax.ShapeDtypeStruct((UNITS, half), F32),
+        ),
+        in_specs=[hbm] * 5,
+        out_specs=(hbm,) * 3,
+        scratch_shapes=list(scratch.values()),
+        compiler_params=pltpu.CompilerParams(
+            collective_id=0, has_side_effects=True, vmem_limit_bytes=VMEM_ASKED
+        ),
+    )(block_in, gain, weight_in, weight_out, output_grad)
+    return pl.pallas_call(
+        finish_kernel,
+        name="finish",
         out_shape=(
             jax.ShapeDtypeStruct((rows, width), BF16),
             jax.ShapeDtypeStruct((rows, width), BF16),
             jax.ShapeDtypeStruct((half, UNITS), F32),
             jax.ShapeDtypeStruct((UNITS, half), F32),
         ),
-        in_specs=[vmem, vmem, hbm, hbm, vmem],
-        out_specs=(vmem, vmem, hbm, hbm),
-        scratch_shapes=list(scratch.values()),
-        compiler_params=pltpu.CompilerParams(
-            collective_id=0, has_side_effects=True, vmem_limit_bytes=58 * 2**20
-        ),
-    )(block_in, norm_gain.reshape(1, width), weight_in, weight_out, output_grad)
+        in_specs=[hbm] * 6,
+        out_specs=(hbm,) * 4,
+        scratch_shapes=[
+            *inputs.values(), buf(2, NX, rows, WIDE, dtype=F32), buf(UNITS, half, dtype=F32),
+            buf(half, UNITS, dtype=F32), buf(UNITS, half, dtype=F32), buf(rows, width),
+            buf(rows, width), pltpu.SemaphoreType.DMA((6,)), pltpu.SemaphoreType.DMA((4,)),
+        ],
+        compiler_params=pltpu.CompilerParams(vmem_limit_bytes=VMEM_ASKED),
+    )(block_in, gain, output_grad, summed, gin_t, gout)
 
 
 def solution(mesh):

time: 112 us -> 107 us (0.955)
  local copies, waits for them, and re-layouts: 6.55 us -> 0 us
  Pallas kernels: 103 us -> 105 us
    unnamed x6 -> x0, local copies, waits for them, and re-layouts: 6.55 us -> none
    pallas_call x1 -> x2, Pallas kernels: 103 us -> 105 us  [the longest x1 102 us: local(): pl.pallas_call(kernel, name='block', out_shape=(jax.ShapeDtypeStruct((2,...]
where the time goes in v3:
time: 107 us; the launch traced here: 106 us
  Pallas kernels  105 us (98%)
    pallas_call x1, Pallas kernels, local(): pl.pallas_call(kernel, name='block', out_shape=(jax.ShapeDtypeStruct((2,...  102 us
    pallas_call x1, Pallas kernels, local(): pl.pallas_call(finish_kernel, name='finish', out_shape=(jax.ShapeDtypeStr...  3.18 us

profile of v3, /device:TPU:1, one launch (start us, length us, event | category | flops | bytes accessed | tf_op | source)
XLA Modules:
  0.0 106.1 jit_solution(6651428435682757316)
XLA Ops:
  0.6 102.1 %block.1 = (f32[2,4,8,1536]{3,2,1,0:T(8,128)}, f32[384,768]{1,0:T(8,128)}, f32[384,768]{1,0:T(8,128)}) custom-call(bf16[8,6144]{1,0:T(8,128)(2,1)} %x_any.3, f32[1,6144]{1,0:T(1,128)} %bitcast.1, bf16[6144,384]{1,0:T(8,128)(2,1)} %wi_any.1, bf16[384,6144]{1,0:T(8,128)(2,1)} %wo_any.1, bf16[8,6144]{1,0:T(8,128)(2,1)} %g_any.3), custom_call_target="tpu_custom_call" | custom-call | tf_op jit(solution)/shard_map/block/pallas_call | solution.py:536
  102.7 3.2 %finish.1 = (bf16[8,6144]{1,0:T(8,128)(2,1)}, bf16[8,6144]{1,0:T(8,128)(2,1)}, f32[768,384]{1,0:T(8,128)}, f32[384,768]{1,0:T(8,128)}) custom-call(bf16[8,6144]{1,0:T(8,128)(2,1)} %x_any.3, f32[1,6144]{1,0:T(1,128)} %bitcast.2, bf16[8,6144]{1,0:T(8,128)(2,1)} %g_any.3, f32[2,4,8,1536]{3,2,1,0:T(8,128)} %get-tuple-element.7.rows_any, ...), custom_call_target="tpu_custom_call" | custom-call | tf_op jit(solution)/shard_map/finish/pallas_call | solution.py:551

commit v4 on v3

--- a/solution.py
+++ b/solution.py
@@ -14,9 +14,10 @@
 WIDE = 1536
 UNITS = 384
 BLOCK = 256
-HALF = CHUNK // 2
-PER = BLOCK // (4 * HALF)
-FAR = 3
+SIDE = WIDE // 2
+UNIT = 2 * ROWS
+PER = BLOCK // (4 * CHUNK)
+FAR = 4
 SEMS = 320
 VMEM_ASKED = 60 * 2**20
 
@@ -102,9 +103,9 @@
     rows_any, gin_any, gout_any,
     x_ref, gain_ref, g_ref, wi, wo, msg, got, acts, cots,
     terms, terms_in, slope, hid, dpre, hid_t, dpre_t,
-    prod, prod_sib, ring_in, ring_out, y_out, y_in, rows_out, rows_in,
+    prod, prod_sib, ring_in, ring_out, y_out, y_in, rows_out,
     gsum, gsend, gin_got, gres,
-    ssem, rsem, lsem,
+    ssem, rsem, lsem, ksem,
 ):
     x, yl, yh, z, c = place()
     xs = [lax.rem(x + k, NX) for k in range(NX)]
@@ -119,17 +120,19 @@
     for other in (*to_z, to_sib, to_yh, to_yl, *to_x[1:]):
         pl.semaphore_signal(barrier, inc=1, device_id=other, device_id_type=MESH)
 
-    load_wi = pltpu.make_async_copy(
-        wi_any.at[pl.ds(pl.multiple_of(x * WIDE, WIDE), WIDE)], wi, lsem.at[0])
-    load_wo = pltpu.make_async_copy(
-        wo_any.at[:, pl.ds(pl.multiple_of(x * WIDE, WIDE), WIDE)], wo, lsem.at[1])
+    weights = []
+    for a in range(NX):
+        cols = pl.ds(a * WIDE, WIDE)
+        weights.append(pltpu.make_async_copy(wi_any.at[cols], wi.at[a], lsem.at[5 + a]))
+        weights.append(pltpu.make_async_copy(wo_any.at[:, cols], wo.at[a], lsem.at[9 + a]))
+
     loads = [
-        pltpu.make_async_copy(src, dst, lsem.at[4 + k])
+        pltpu.make_async_copy(src, dst, lsem.at[2 + k])
         for k, (src, dst) in enumerate(((x_any, x_ref), (gain_any, gain_ref), (g_any, g_ref)))]
     for copy in loads:
         copy.start()
-    load_wi.start()
-    load_wo.start()
+    for copy in weights:
+        copy.start()
     for copy in loads:
         copy.wait()
 
@@ -158,9 +161,9 @@
         copy.wait_recv()
     pieces = [got[a].astype(F32) for a in range(NX)]
     for part in (0, 1):
-        pair = pieces[2 * part:2 * part + 2]
-        acts[part, 0] = jnp.concatenate([p[:ROWS] for p in pair], axis=0).astype(BF16)
-        cots[part, 0] = jnp.concatenate([p[ROWS:] for p in pair], axis=0).astype(BF16)
+        cols = slice(part * SIDE, (part + 1) * SIDE)
+        acts[part, 0] = jnp.concatenate([p[:ROWS, cols] for p in pieces], axis=0).astype(BF16)
+        cots[part, 0] = jnp.concatenate([p[ROWS:, cols] for p in pieces], axis=0).astype(BF16)
 
     def ways(dist, part, turn):
         return (0, 1) if dist < 4 else (part ^ turn,)
@@ -213,10 +216,12 @@
                 self.y[part, way, dist].wait_recv()
                 self.to_core(part, slot(way, dist))
 
-        def block(self, part, b):
+        def block(self, b):
             for s in range(PER * b, PER * b + PER):
-                self.sib[part, s].wait_recv()
-            return self.buf[part, 4 * PER * b:4 * PER * (b + 1)].reshape(BLOCK, WIDE)
+                for part in (0, 1):
+                    self.sib[part, s].wait_recv()
+            return [
+                self.buf[part, 8 * b:8 * b + 8].reshape(BLOCK, SIDE) for part in (0, 1)]
 
     class Across:
         def __init__(self, i, result):
@@ -224,7 +229,9 @@
             self.out, self.back = {}, {}
 
         def give(self, b, term):
-            self.term[b] = term.astype(BF16).reshape(NX, BLOCK // NX, UNITS)
+            term = term.reshape(8, NX, ROWS, UNITS)
+            for q in range(NX):
+                self.term[b, q] = term[:, q].reshape(8 * ROWS, UNITS).astype(BF16)
             self.out[b] = [
                 send(self.term.at[b, xs[k]], self.came.at[b, k - 1], to_x[k]) for k in range(1, NX)]
 
@@ -241,10 +248,15 @@
             self.back[b] = [
                 send(self.result.at[b, x], self.result.at[b, x], to_x[k]) for k in range(1, NX)]
 
-        def whole(self, b):
+        def own(self):
+            return self.result[:, x].reshape(BLOCK, UNITS)
+
+        def turned(self, b):
             for copy in self.back[b]:
                 copy.wait_recv()
-            return self.result[b].reshape(BLOCK, UNITS)
+            value = self.result[b].astype(F32).reshape(NX, 8, ROWS, UNITS)
+            rows = [value[q, k] for k in range(8) for q in range(NX)]
+            return jnp.concatenate(rows, axis=0).T.astype(BF16)
 
     class Scatter:
         def __init__(self, i, turn):
@@ -252,26 +264,34 @@
             self.prod, self.sib = prod.at[i], prod_sib.at[i]
             self.rin, self.rout = ring_in.at[i], ring_out.at[i]
             self.yout, self.yin = y_out.at[i], y_in.at[i]
-            self.xout, self.xin = rows_out.at[i], rows_in.at[i]
+            self.rows_out, self.rows_hbm = rows_out.at[i], rows_any.at[i]
             self.sibs, self.ring, self.y, self.seen = {}, {}, {}, set()
-
-        def give(self, k, left, right, dims):
+            self.keep, self.keep_sem = {}, ksem.at[i]
+
+        def give(self, part, left, right, turned):
             for n in range(0, WIDE, 512):
-                if dims == 1:
-                    term = dot(left, right[n:n + 512, :], ((1,), (1,)))
-                else:
-                    term = dot(left, right[:, n:n + 512])
-                term = term.astype(BF16).reshape(PER, 2, 2, HALF, 512)
+                pair = []
+                for a in (2 * part, 2 * part + 1):
+                    if turned:
+                        term = dot(left, right[a, n:n + 512, :], ((1,), (1,)))
+                    else:
+                        term = dot(left, right[a, :, n:n + 512])
+                    pair.append(term.reshape(NZ, 2, 2, ROWS, 512))
+                term = jnp.concatenate(pair, axis=3).astype(BF16)
                 for core in (0, 1):
-                    self.prod[core, k, :, :, n:n + 512] = term[:, core].reshape(2 * PER, HALF, 512)
-            self.sibs[k] = send(self.prod.at[1, k], self.sib.at[k], to_sib)
+                    rows = term[:, core].reshape(2 * NZ, UNIT, 512)
+                    self.prod[core, part, :, :, n:n + 512] = rows
+            for k in (1, 0):
+                rows = pl.ds(NZ * k, NZ)
+                self.sibs[part, k] = send(
+                    self.prod.at[1, part, rows], self.sib.at[part, rows], to_sib)
 
         def term(self, part, s, h):
-            k, q = 2 * part + s // PER, 2 * (s % PER) + h
-            if k not in self.seen:
-                self.seen.add(k)
-                self.sibs[k].wait_recv()
-            return self.prod[0, k, q].astype(F32) + self.sib[k, q].astype(F32)
+            k, q = s // 4, 2 * s + h
+            if (part, k) not in self.seen:
+                self.seen.add((part, k))
+                self.sibs[part, k].wait_recv()
+            return self.prod[0, part, q].astype(F32) + self.sib[part, q].astype(F32)
 
         def hop(self, part, way, dist, h):
             value = self.term(part, slot(way, dist), h)
@@ -302,15 +322,11 @@
             value = self.near(part, 0)
             self.y[part].wait_recv()
             value = value + self.yin[part].astype(F32)
-            self.xout[2 * part:2 * part + 2] = value.reshape(2, ROWS, WIDE)
-
-        def across(self):
-            self.x = [send(self.xout.at[xs[k]], self.xin.at[x], to_x[k]) for k in range(1, NX)]
-            self.xin[x] = self.xout[x]
-
-        def done(self):
-            for copy in self.x:
-                copy.wait_recv()
+            self.rows_out[2 * part:2 * part + 2] = value.reshape(2, ROWS, WIDE)
+            cols = pl.ds(2 * part, 2)
+            self.keep[part] = pltpu.make_async_copy(
+                self.rows_out.at[cols], self.rows_hbm.at[cols], self.keep_sem.at[part])
+            self.keep[part].start()
 
     class Weights:
         def __init__(self, i):
@@ -319,9 +335,9 @@
         def give(self, left_t, right):
             left = left_t[...]
             for n in range(4):
-                cols = slice(n * UNITS, (n + 1) * UNITS)
-                term = dot(left, right[:, :, :, cols].reshape(4 * BLOCK, UNITS))
-                self.sum[n // 2, :, (n % 2) * UNITS:(n % 2 + 1) * UNITS] = term
+                cols = slice((n % 2) * UNITS, (n % 2 + 1) * UNITS)
+                term = dot(left, right[n // 2, :, :, cols].reshape(4 * BLOCK, UNITS))
+                self.sum[n // 2, :, cols] = term
             self.out[...] = self.sum[1 - yl].astype(BF16)
             self.copy = send(self.out, self.came, to_yl)
 
@@ -334,38 +350,34 @@
     out, back = Scatter(0, 0), Scatter(1, 1)
     w_out, w_in = Weights(0), Weights(1)
 
-    def pre(part, b):
-        fwd.give(2 * part + b, dot(ga.block(part, b), wi[...]))
-
-    def act(part, b):
-        k = 2 * part + b
-        value = fwd.total(k)
+    def pre(b):
+        sides = ga.block(b)
+        fwd.give(b, dot(sides[0], wi[x, :SIDE]) + dot(sides[1], wi[x, SIDE:]))
+
+    def act(b):
+        value = fwd.total(b)
         cdf = 0.5 * (1.0 + lax.erf(value * 0.7071067811865476))
-        slope[k] = cdf + value * jnp.exp(-0.5 * value * value) * 0.3989422804014327
-        fwd.share(k, value * cdf)
-
-    def cot(part, b):
-        bwd.give(2 * part + b, dot(gg.block(part, b), wo[...], ((1,), (1,))))
-
-    def act_back(part, b):
-        k = 2 * part + b
-        bwd.share(k, bwd.total(k) * slope[k])
-
-    def branch(part, b):
-        k = 2 * part + b
-        value = fwd.whole(k)
-        hid_t[:, k * BLOCK:(k + 1) * BLOCK] = value.T
-        out.give(k, value, wo, 0)
-
-    def back_prod(part, b):
-        k = 2 * part + b
-        value = bwd.whole(k)
-        dpre_t[:, k * BLOCK:(k + 1) * BLOCK] = value.T
-        back.give(k, value, wi, 1)
-
-    def mixed():
-        out.done()
-        keep_out.start()
+        slope[b] = cdf + value * jnp.exp(-0.5 * value * value) * 0.3989422804014327
+        fwd.share(b, value * cdf)
+
+    def cot(b):
+        sides, dims = gg.block(b), ((1,), (1,))
+        bwd.give(b, dot(sides[0], wo[x, :, :SIDE], dims) + dot(sides[1], wo[x, :, SIDE:], dims))
+
+    def act_back(b):
+        bwd.share(b, bwd.total(b) * slope[b])
+
+    def branch(part):
+        out.give(part, fwd.own(), wo, False)
+
+    def back_prod(part):
+        back.give(part, bwd.own(), wi, True)
+
+    def turn(b):
+        hid_t[:, b * BLOCK:(b + 1) * BLOCK] = fwd.turned(b)
+
+    def turn_back(b):
+        dpre_t[:, b * BLOCK:(b + 1) * BLOCK] = bwd.turned(b)
 
     def store_out_grad():
         gres[0] = w_out.total()
@@ -375,133 +387,127 @@
         gres[1] = w_in.total()
         store_in.start()
 
-    def finish():
-        back.done()
-        keep_back.start()
-
-    store_out = pltpu.make_async_copy(gres.at[0], gout_any, lsem.at[2])
-    store_in = pltpu.make_async_copy(gres.at[1], gin_any, lsem.at[3])
-    keep_out = pltpu.make_async_copy(rows_in.at[0], rows_any.at[0], lsem.at[7])
-    keep_back = pltpu.make_async_copy(rows_in.at[1], rows_any.at[1], lsem.at[8])
-
+    store_out = pltpu.make_async_copy(gres.at[0], gout_any, lsem.at[0])
+    store_in = pltpu.make_async_copy(gres.at[1], gin_any, lsem.at[1])
+
+    ga.start(1)
     ga.start(0)
-    ga.start(1)
+    ga.own(1, 1)
     ga.own(0, 1)
     ga.other(0)
-    ga.own(1, 1)
     ga.other(1)
+    ga.own(1, 2)
     ga.own(0, 2)
     ga.oth(0, 1)
+    ga.oth(1, 1)
+    ga.own(1, 3)
+    ga.own(0, 3)
     gg.start(0)
-    ga.own(1, 2)
     gg.start(1)
-    ga.oth(1, 1)
-    ga.own(0, 3)
+    for copy in weights:
+        copy.wait()
+    pre(0)
     ga.oth(0, 2)
-    load_wi.wait()
-    load_wo.wait()
-    pre(0, 0)
+    ga.oth(1, 2)
+    pre(1)
+    gg.own(0, 1)
+    gg.other(1)
+    ga.own(0, 4)
+    ga.own(1, 4)
+    gg.own(1, 1)
     gg.other(0)
-    gg.own(0, 1)
-    ga.own(1, 3)
-    gg.other(1)
-    gg.own(1, 1)
-    ga.far(0, 3)
-    ga.oth(1, 2)
-    ga.own(0, 4)
+    ga.oth(0, 3)
+    act(0)
+    ga.oth(1, 3)
+    pre(2)
+    gg.own(0, 2)
+    ga.far(0, 4)
+    gg.oth(1, 1)
+    gg.own(1, 2)
+    ga.far(1, 4)
+    pre(3)
+    gg.own(0, 3)
     gg.oth(0, 1)
-    act(0, 0)
-    ga.far(1, 3)
-    gg.own(0, 2)
-    pre(1, 0)
-    ga.own(1, 4)
-    gg.oth(1, 1)
-    ga.far(0, 4)
-    gg.own(1, 2)
-    pre(0, 1)
-    branch(0, 0)
-    ga.far(1, 4)
-    act(1, 0)
-    gg.own(0, 3)
+    cot(0)
+    act(2)
     gg.oth(1, 2)
     gg.own(1, 3)
-    pre(1, 1)
-    cot(1, 0)
     gg.own(0, 4)
+    act(1)
+    gg.oth(0, 2)
+    act(3)
+    branch(1)
+    branch(0)
+    out.hops(0, 4, 1)
+    out.hops(0, 4, 0)
+    out.hops(1, 4, 0)
+    out.hops(1, 4, 1)
     gg.own(1, 4)
-    branch(1, 0)
-    gg.far(0, 3)
-    act(0, 1)
-    gg.oth(0, 2)
-    act(1, 1)
-    gg.far(1, 3)
-    cot(0, 0)
-    act_back(1, 0)
+    cot(1)
+    gg.oth(0, 3)
+    gg.oth(1, 3)
+    turn(2)
+    act_back(0)
+    turn(0)
+    turn(3)
+    gg.far(0, 4)
+    cot(2)
+    out.hops(0, 3, 1)
+    out.hops(1, 3, 0)
     gg.far(1, 4)
-    gg.far(0, 4)
-    branch(0, 1)
-    cot(0, 1)
-    cot(1, 1)
-    branch(1, 1)
+    cot(3)
+    out.hops(1, 3, 1)
+    out.hops(0, 3, 0)
+    act_back(1)
+    out.hops(0, 2, 1)
+    turn(1)
     w_out.give(hid_t, cots)
-    out.hops(1, 4, 1)
-    out.hops(1, 4, 0)
-    out.hops(0, 4, 0)
-    out.hops(0, 4, 1)
-    act_back(0, 0)
-    back_prod(1, 0)
-    act_back(0, 1)
-    out.hops(0, 3, 0)
-    act_back(1, 1)
-    out.hops(0, 3, 1)
-    out.hops(1, 3, 1)
-    out.hops(1, 3, 0)
-    back_prod(0, 0)
+    out.hops(1, 2, 1)
+    act_back(3)
     out.hops(0, 2, 0)
-    back_prod(0, 1)
-    out.hops(0, 2, 1)
-    out.hops(1, 2, 1)
-    back_prod(1, 1)
+    out.hops(0, 1, 1)
+    turn_back(0)
+    turn_back(1)
+    out.hops(1, 1, 1)
+    out.hops(1, 2, 0)
+    out.hops(0, 1, 0)
+    turn_back(3)
+    out.cross(0)
+    act_back(2)
+    back_prod(1)
+    back_prod(0)
+    back.hops(1, 4, 0)
     back.hops(0, 4, 1)
+    turn_back(2)
+    back.hops(1, 4, 1)
+    w_in.give(dpre_t, acts)
     back.hops(0, 4, 0)
-    out.hops(0, 1, 0)
-    out.hops(0, 1, 1)
-    back.hops(1, 4, 1)
-    out.hops(1, 2, 0)
-    out.hops(1, 1, 1)
-    back.hops(1, 4, 0)
-    w_in.give(dpre_t, acts)
+    back.hops(0, 3, 1)
+    back.hops(1, 3, 1)
     back.hops(0, 3, 0)
-    back.hops(0, 3, 1)
-    store_out_grad()
-    back.hops(1, 3, 1)
-    back.hops(1, 3, 0)
-    out.hops(1, 1, 0)
     back.hops(0, 2, 1)
     back.hops(1, 2, 1)
-    back.hops(1, 2, 0)
-    out.cross(0)
-    out.cross(1)
-    back.hops(0, 2, 0)
+    back.hops(1, 3, 0)
     back.hops(0, 1, 1)
     back.hops(1, 1, 1)
+    back.hops(0, 2, 0)
+    back.hops(1, 2, 0)
+    back.cross(0)
+    back.hops(0, 1, 0)
+    out.cross(1)
+    out.hops(1, 1, 0)
+    back.cross(1)
     back.hops(1, 1, 0)
-    back.hops(0, 1, 0)
-    back.cross(0)
-    back.cross(1)
+    out.rows(0)
+    store_out_grad()
     store_in_grad()
-    out.rows(0)
+    back.rows(0)
     out.rows(1)
-    out.across()
-    back.rows(0)
     back.rows(1)
-    back.across()
-    mixed()
-    finish()
 
     for copy in pending:
         copy.wait_send()
-    for copy in (store_out, store_in, keep_out, keep_back):
+    for copy in (store_out, store_in, *out.keep.values(), *back.keep.values()):
         copy.wait()
 
 
@@ -517,21 +523,21 @@
     quarter = BLOCK // NX
     inputs = dict(x=buf(rows, width), gain=buf(1, width, dtype=F32), g=buf(rows, width))
     scratch = dict(
-        **inputs, wi=buf(WIDE, UNITS), wo=buf(UNITS, WIDE),
+        **inputs, wi=buf(NX, WIDE, UNITS), wo=buf(NX, UNITS, WIDE),
         msg=buf(NX, 2 * ROWS, WIDE), got=buf(NX, 2 * ROWS, WIDE),
-        acts=buf(2, 32, HALF, WIDE), cots=buf(2, 32, HALF, WIDE),
+        acts=buf(2, 32, CHUNK, SIDE), cots=buf(2, 32, CHUNK, SIDE),
         terms=buf(2, 4, NX, quarter, UNITS), terms_in=buf(2, 4, NX - 1, quarter, UNITS),
         slope=buf(4, quarter, UNITS, dtype=F32),
         hid=buf(4, NX, quarter, UNITS), dpre=buf(4, NX, quarter, UNITS),
         hid_t=buf(UNITS, 4 * BLOCK), dpre_t=buf(UNITS, 4 * BLOCK),
-        prod=buf(2, 2, 4, 2 * PER, HALF, WIDE), prod_sib=buf(2, 4, 2 * PER, HALF, WIDE),
-        ring_in=buf(2, 2, 2, 4, 2, HALF, WIDE), ring_out=buf(2, 2, 2, 4, 2, HALF, WIDE),
-        y_out=buf(2, 2, HALF, WIDE), y_in=buf(2, 2, HALF, WIDE),
-        rows_out=buf(2, NX, ROWS, WIDE, dtype=F32), rows_in=buf(2, NX, ROWS, WIDE, dtype=F32),
+        prod=buf(2, 2, 2, 2 * NZ, UNIT, WIDE), prod_sib=buf(2, 2, 2 * NZ, UNIT, WIDE),
+        ring_in=buf(2, 2, 2, 4, 2, UNIT, WIDE), ring_out=buf(2, 2, 2, 4, 2, UNIT, WIDE),
+        y_out=buf(2, 2, UNIT, WIDE), y_in=buf(2, 2, UNIT, WIDE),
+        rows_out=buf(2, NX, ROWS, WIDE, dtype=F32),
         gsum=buf(2, 2, UNITS, half, dtype=F32), gsend=buf(2, UNITS, half),
         gin_got=buf(2, UNITS, half), gres=buf(2, UNITS, half, dtype=F32),
         ssem=pltpu.SemaphoreType.DMA((SEMS,)), rsem=pltpu.SemaphoreType.DMA((SEMS,)),
-        lsem=pltpu.SemaphoreType.DMA((9,)),
+        lsem=pltpu.SemaphoreType.DMA((13,)), ksem=pltpu.SemaphoreType.DMA((2, 2)),
     )
     summed, gin_t, gout = pl.pallas_call(
         kernel,

time: 107 us -> 99.3 us (0.928)
  Pallas kernels: 105 us -> 98.4 us
    pallas_call x1, Pallas kernels: 102 us -> 95.2 us  [local(): pl.pallas_call(kernel, name='block', out_shape=(jax.ShapeDtypeStruct((2,...]
where the time goes in v4:
time: 99.3 us; the launch traced here: 99.2 us
  Pallas kernels  98.4 us (99%)
    pallas_call x1, Pallas kernels, local(): pl.pallas_call(kernel, name='block', out_shape=(jax.ShapeDtypeStruct((2,...  95.2 us
    pallas_call x1, Pallas kernels, local(): pl.pallas_call(finish_kernel, name='finish', out_shape=(jax.ShapeDtypeStr...  3.18 us

profile of v4, /device:TPU:1, one launch (start us, length us, event | category | flops | bytes accessed | tf_op | source)
XLA Modules:
  0.0 99.2 jit_solution(9760947989718914999)
XLA Ops:
  0.6 95.2 %block.1 = (f32[2,4,8,1536]{3,2,1,0:T(8,128)}, f32[384,768]{1,0:T(8,128)}, f32[384,768]{1,0:T(8,128)}) custom-call(bf16[8,6144]{1,0:T(8,128)(2,1)} %x_any.3, f32[1,6144]{1,0:T(1,128)} %bitcast.1, bf16[6144,384]{1,0:T(8,128)(2,1)} %wi_any.1, bf16[384,6144]{1,0:T(8,128)(2,1)} %wo_any.1, bf16[8,6144]{1,0:T(8,128)(2,1)} %g_any.3), custom_call_target="tpu_custom_call" | custom-call | tf_op jit(solution)/shard_map/block/pallas_call | solution.py:542
  95.9 3.2 %finish.1 = (bf16[8,6144]{1,0:T(8,128)(2,1)}, bf16[8,6144]{1,0:T(8,128)(2,1)}, f32[768,384]{1,0:T(8,128)}, f32[384,768]{1,0:T(8,128)}) custom-call(bf16[8,6144]{1,0:T(8,128)(2,1)} %x_any.3, f32[1,6144]{1,0:T(1,128)} %bitcast.2, bf16[8,6144]{1,0:T(8,128)(2,1)} %g_any.3, f32[2,4,8,1536]{3,2,1,0:T(8,128)} %get-tuple-element.7.rows_any, ...), custom_call_target="tpu_custom_call" | custom-call | tf_op jit(solution)/shard_map/finish/pallas_call | solution.py:557

commit v5 on v4

--- a/solution.py
+++ b/solution.py
@@ -243,8 +243,10 @@
                 total = total + self.came[b, k].astype(F32)
             return total
 
-        def share(self, b, value):
+        def keep(self, b, value):
             self.result[b, x] = value.astype(BF16)
+
+        def share(self, b):
             self.back[b] = [
                 send(self.result.at[b, x], self.result.at[b, x], to_x[k]) for k in range(1, NX)]
 
@@ -358,14 +360,14 @@
         value = fwd.total(b)
         cdf = 0.5 * (1.0 + lax.erf(value * 0.7071067811865476))
         slope[b] = cdf + value * jnp.exp(-0.5 * value * value) * 0.3989422804014327
-        fwd.share(b, value * cdf)
+        fwd.keep(b, value * cdf)
 
     def cot(b):
         sides, dims = gg.block(b), ((1,), (1,))
         bwd.give(b, dot(sides[0], wo[x, :, :SIDE], dims) + dot(sides[1], wo[x, :, SIDE:], dims))
 
     def act_back(b):
-        bwd.share(b, bwd.total(b) * slope[b])
+        bwd.keep(b, bwd.total(b) * slope[b])
 
     def branch(part):
         out.give(part, fwd.own(), wo, False)
@@ -392,117 +394,125 @@
 
     ga.start(1)
     ga.start(0)
+    gg.start(0)
     ga.own(1, 1)
     ga.own(0, 1)
+    ga.other(1)
     ga.other(0)
-    ga.other(1)
     ga.own(1, 2)
     ga.own(0, 2)
+    ga.oth(1, 1)
     ga.oth(0, 1)
-    ga.oth(1, 1)
     ga.own(1, 3)
-    ga.own(0, 3)
-    gg.start(0)
     gg.start(1)
     for copy in weights:
         copy.wait()
     pre(0)
+    ga.own(0, 3)
+    ga.oth(1, 2)
     ga.oth(0, 2)
-    ga.oth(1, 2)
+    gg.own(0, 1)
+    ga.own(1, 4)
+    gg.other(1)
     pre(1)
-    gg.own(0, 1)
-    gg.other(1)
     ga.own(0, 4)
-    ga.own(1, 4)
-    gg.own(1, 1)
-    gg.other(0)
-    ga.oth(0, 3)
     act(0)
     ga.oth(1, 3)
+    gg.own(1, 1)
+    fwd.share(0)
+    ga.oth(0, 3)
+    gg.other(0)
+    gg.own(0, 2)
+    ga.far(1, 4)
     pre(2)
-    gg.own(0, 2)
     ga.far(0, 4)
+    act(1)
+    gg.own(1, 2)
     gg.oth(1, 1)
-    gg.own(1, 2)
-    ga.far(1, 4)
     pre(3)
+    fwd.share(1)
     gg.own(0, 3)
     gg.oth(0, 1)
+    gg.own(1, 3)
+    act(2)
+    turn(0)
+    fwd.share(2)
+    gg.oth(1, 2)
+    gg.own(0, 4)
+    act(3)
+    fwd.share(3)
+    branch(0)
+    gg.own(1, 4)
+    gg.oth(0, 2)
+    branch(1)
     cot(0)
-    act(2)
-    gg.oth(1, 2)
-    gg.own(1, 3)
-    gg.own(0, 4)
-    act(1)
-    gg.oth(0, 2)
-    act(3)
-    branch(1)
-    branch(0)
     out.hops(0, 4, 1)
-    out.hops(0, 4, 0)
-    out.hops(1, 4, 0)
-    out.hops(1, 4, 1)
-    gg.own(1, 4)
+    gg.oth(1, 3)
+    gg.far(0, 4)
+    turn(2)
     cot(1)
     gg.oth(0, 3)
-    gg.oth(1, 3)
-    turn(2)
-    act_back(0)
-    turn(0)
     turn(3)
-    gg.far(0, 4)
+    gg.far(1, 4)
+    turn(1)
+    out.hops(1, 4, 1)
     cot(2)
     out.hops(0, 3, 1)
+    cot(3)
+    w_out.give(hid_t, cots)
+    out.hops(1, 4, 0)
+    out.hops(0, 4, 0)
+    act_back(0)
+    act_back(1)
+    bwd.share(0)
+    out.hops(1, 3, 1)
+    act_back(2)
+    out.hops(0, 2, 1)
+    bwd.share(2)
+    act_back(3)
+    bwd.share(3)
+    out.hops(0, 3, 0)
     out.hops(1, 3, 0)
-    gg.far(1, 4)
-    cot(3)
-    out.hops(1, 3, 1)
-    out.hops(0, 3, 0)
-    act_back(1)
-    out.hops(0, 2, 1)
-    turn(1)
-    w_out.give(hid_t, cots)
+    back_prod(0)
+    bwd.share(1)
+    out.hops(0, 1, 1)
+    back_prod(1)
     out.hops(1, 2, 1)
-    act_back(3)
+    turn_back(0)
+    back.hops(0, 4, 1)
+    back.hops(0, 4, 0)
     out.hops(0, 2, 0)
-    out.hops(0, 1, 1)
-    turn_back(0)
+    turn_back(2)
+    out.cross(0)
+    back.hops(1, 4, 0)
+    back.hops(1, 4, 1)
+    out.hops(1, 2, 0)
+    turn_back(3)
     turn_back(1)
-    out.hops(1, 1, 1)
-    out.hops(1, 2, 0)
-    out.hops(0, 1, 0)
-    turn_back(3)
-    out.cross(0)
-    act_back(2)
-    back_prod(1)
-    back_prod(0)
-    back.hops(1, 4, 0)
-    back.hops(0, 4, 1)
-    turn_back(2)
-    back.hops(1, 4, 1)
     w_in.give(dpre_t, acts)
-    back.hops(0, 4, 0)
     back.hops(0, 3, 1)
     back.hops(1, 3, 1)
     back.hops(0, 3, 0)
+    out.hops(0, 1, 0)
     back.hops(0, 2, 1)
+    out.hops(1, 1, 1)
     back.hops(1, 2, 1)
     back.hops(1, 3, 0)
+    back.hops(0, 2, 0)
+    store_out_grad()
     back.hops(0, 1, 1)
+    out.cross(1)
     back.hops(1, 1, 1)
-    back.hops(0, 2, 0)
     back.hops(1, 2, 0)
+    out.hops(1, 1, 0)
+    back.hops(0, 1, 0)
     back.cross(0)
-    back.hops(0, 1, 0)
-    out.cross(1)
-    out.hops(1, 1, 0)
+    out.rows(0)
     back.cross(1)
     back.hops(1, 1, 0)
-    out.rows(0)
-    store_out_grad()
+    out.rows(1)
     store_in_grad()
     back.rows(0)
-    out.rows(1)
     back.rows(1)
 
     for copy in pending:

time: 99.3 us -> 95.8 us (0.965)
  Pallas kernels: 98.4 us -> 94.8 us
    pallas_call x1, Pallas kernels: 95.2 us -> 91.6 us  [local(): pl.pallas_call(kernel, name='block', out_shape=(jax.ShapeDtypeStruct((2,...]
where the time goes in v5:
time: 95.8 us; the launch traced here: 95.6 us
  Pallas kernels  94.8 us (99%)
    pallas_call x1, Pallas kernels, local(): pl.pallas_call(kernel, name='block', out_shape=(jax.ShapeDtypeStruct((2,...  91.6 us
    pallas_call x1, Pallas kernels, local(): pl.pallas_call(finish_kernel, name='finish', out_shape=(jax.ShapeDtypeStr...  3.18 us

profile of v5, /device:TPU:1, one launch (start us, length us, event | category | flops | bytes accessed | tf_op | source)
XLA Modules:
  0.0 95.6 jit_solution(12748062457845791280)
XLA Ops:
  0.6 91.6 %block.1 = (f32[2,4,8,1536]{3,2,1,0:T(8,128)}, f32[384,768]{1,0:T(8,128)}, f32[384,768]{1,0:T(8,128)}) custom-call(bf16[8,6144]{1,0:T(8,128)(2,1)} %x_any.3, f32[1,6144]{1,0:T(1,128)} %bitcast.1, bf16[6144,384]{1,0:T(8,128)(2,1)} %wi_any.1, bf16[384,6144]{1,0:T(8,128)(2,1)} %wo_any.1, bf16[8,6144]{1,0:T(8,128)(2,1)} %g_any.3), custom_call_target="tpu_custom_call" | custom-call | tf_op jit(solution)/shard_map/block/pallas_call | solution.py:552
  92.3 3.2 %finish.1 = (bf16[8,6144]{1,0:T(8,128)(2,1)}, bf16[8,6144]{1,0:T(8,128)(2,1)}, f32[768,384]{1,0:T(8,128)}, f32[384,768]{1,0:T(8,128)}) custom-call(bf16[8,6144]{1,0:T(8,128)(2,1)} %x_any.3, f32[1,6144]{1,0:T(1,128)} %bitcast.2, bf16[8,6144]{1,0:T(8,128)(2,1)} %g_any.3, f32[2,4,8,1536]{3,2,1,0:T(8,128)} %get-tuple-element.7.rows_any, ...), custom_call_target="tpu_custom_call" | custom-call | tf_op jit(solution)/shard_map/finish/pallas_call | solution.py:567

commit v6 on v5

--- a/solution.py
+++ b/solution.py
@@ -17,7 +17,7 @@
 SIDE = WIDE // 2
 UNIT = 2 * ROWS
 PER = BLOCK // (4 * CHUNK)
-FAR = 4
+FAR = 3
 SEMS = 320
 VMEM_ASKED = 60 * 2**20
 
@@ -394,125 +394,125 @@
 
     ga.start(1)
     ga.start(0)
-    gg.start(0)
+    gg.start(1)
     ga.own(1, 1)
     ga.own(0, 1)
     ga.other(1)
-    ga.other(0)
     ga.own(1, 2)
     ga.own(0, 2)
+    ga.other(0)
+    gg.start(0)
+    ga.own(1, 3)
+    ga.own(0, 3)
     ga.oth(1, 1)
     ga.oth(0, 1)
-    ga.own(1, 3)
-    gg.start(1)
+    gg.own(1, 1)
+    ga.own(1, 4)
+    ga.own(0, 4)
+    gg.own(0, 1)
+    ga.oth(1, 2)
     for copy in weights:
         copy.wait()
     pre(0)
-    ga.own(0, 3)
-    ga.oth(1, 2)
     ga.oth(0, 2)
-    gg.own(0, 1)
-    ga.own(1, 4)
     gg.other(1)
+    ga.far(1, 3)
+    gg.own(1, 2)
+    ga.far(0, 3)
     pre(1)
-    ga.own(0, 4)
-    act(0)
-    ga.oth(1, 3)
-    gg.own(1, 1)
-    fwd.share(0)
-    ga.oth(0, 3)
-    gg.other(0)
     gg.own(0, 2)
     ga.far(1, 4)
     pre(2)
     ga.far(0, 4)
-    act(1)
-    gg.own(1, 2)
+    gg.other(0)
+    act(0)
+    gg.own(1, 3)
     gg.oth(1, 1)
     pre(3)
+    fwd.share(0)
+    gg.own(0, 3)
+    act(1)
+    gg.oth(0, 1)
+    act(2)
+    gg.own(1, 4)
     fwd.share(1)
-    gg.own(0, 3)
-    gg.oth(0, 1)
-    gg.own(1, 3)
-    act(2)
-    turn(0)
-    fwd.share(2)
     gg.oth(1, 2)
     gg.own(0, 4)
+    fwd.share(2)
     act(3)
     fwd.share(3)
+    branch(1)
+    gg.far(1, 3)
+    gg.oth(0, 2)
+    cot(0)
     branch(0)
-    gg.own(1, 4)
-    gg.oth(0, 2)
-    branch(1)
-    cot(0)
+    turn(0)
+    out.hops(1, 4, 1)
+    turn(1)
+    gg.far(0, 3)
+    gg.far(1, 4)
+    cot(1)
     out.hops(0, 4, 1)
-    gg.oth(1, 3)
     gg.far(0, 4)
+    out.hops(0, 4, 0)
     turn(2)
-    cot(1)
-    gg.oth(0, 3)
+    out.hops(1, 4, 0)
+    cot(2)
     turn(3)
-    gg.far(1, 4)
-    turn(1)
-    out.hops(1, 4, 1)
-    cot(2)
-    out.hops(0, 3, 1)
+    out.hops(1, 3, 1)
     cot(3)
     w_out.give(hid_t, cots)
-    out.hops(1, 4, 0)
-    out.hops(0, 4, 0)
+    act_back(1)
+    bwd.share(1)
     act_back(0)
-    act_back(1)
+    out.hops(1, 2, 1)
     bwd.share(0)
-    out.hops(1, 3, 1)
     act_back(2)
-    out.hops(0, 2, 1)
-    bwd.share(2)
+    out.hops(0, 3, 1)
+    out.hops(1, 3, 0)
+    out.hops(0, 3, 0)
     act_back(3)
     bwd.share(3)
-    out.hops(0, 3, 0)
-    out.hops(1, 3, 0)
+    bwd.share(2)
+    back_prod(1)
+    out.hops(1, 1, 1)
     back_prod(0)
-    bwd.share(1)
-    out.hops(0, 1, 1)
-    back_prod(1)
-    out.hops(1, 2, 1)
+    out.hops(0, 2, 1)
+    back.hops(1, 4, 0)
+    out.hops(1, 2, 0)
+    turn_back(1)
+    back.hops(1, 4, 1)
     turn_back(0)
     back.hops(0, 4, 1)
     back.hops(0, 4, 0)
+    turn_back(3)
     out.hops(0, 2, 0)
+    out.cross(1)
+    out.hops(0, 1, 1)
     turn_back(2)
-    out.cross(0)
-    back.hops(1, 4, 0)
-    back.hops(1, 4, 1)
-    out.hops(1, 2, 0)
-    turn_back(3)
-    turn_back(1)
     w_in.give(dpre_t, acts)
     back.hops(0, 3, 1)
     back.hops(1, 3, 1)
     back.hops(0, 3, 0)
-    out.hops(0, 1, 0)
+    store_out_grad()
+    back.hops(1, 3, 0)
+    out.cross(0)
     back.hops(0, 2, 1)
-    out.hops(1, 1, 1)
     back.hops(1, 2, 1)
-    back.hops(1, 3, 0)
+    out.hops(1, 1, 0)
     back.hops(0, 2, 0)
-    store_out_grad()
     back.hops(0, 1, 1)
-    out.cross(1)
     back.hops(1, 1, 1)
     back.hops(1, 2, 0)
-    out.hops(1, 1, 0)
+    out.hops(0, 1, 0)
+    out.rows(1)
+    back.cross(0)
     back.hops(0, 1, 0)
-    back.cross(0)
-    out.rows(0)
     back.cross(1)
     back.hops(1, 1, 0)
-    out.rows(1)
+    out.rows(0)
+    back.rows(0)
     store_in_grad()
-    back.rows(0)
     back.rows(1)
 
     for copy in pending:

time: 95.8 us -> 98.2 us (1.025)
  Pallas kernels: 94.8 us -> 97.3 us
    pallas_call x1, Pallas kernels: 91.6 us -> 94.1 us  [local(): pl.pallas_call(kernel, name='block', out_shape=(jax.ShapeDtypeStruct((2,...]
where the time goes in v6:
time: 98.2 us; the launch traced here: 98.1 us
  Pallas kernels  97.3 us (99%)
    pallas_call x1, Pallas kernels, local(): pl.pallas_call(kernel, name='block', out_shape=(jax.ShapeDtypeStruct((2,...  94.1 us
    pallas_call x1, Pallas kernels, local(): pl.pallas_call(finish_kernel, name='finish', out_shape=(jax.ShapeDtypeStr...  3.18 us

profile of v6, /device:TPU:1, one launch (start us, length us, event | category | flops | bytes accessed | tf_op | source)
XLA Modules:
  0.0 98.1 jit_solution(2129488153983393095)
XLA Ops:
  0.6 94.1 %block.1 = (f32[2,4,8,1536]{3,2,1,0:T(8,128)}, f32[384,768]{1,0:T(8,128)}, f32[384,768]{1,0:T(8,128)}) custom-call(bf16[8,6144]{1,0:T(8,128)(2,1)} %x_any.3, f32[1,6144]{1,0:T(1,128)} %bitcast.1, bf16[6144,384]{1,0:T(8,128)(2,1)} %wi_any.1, bf16[384,6144]{1,0:T(8,128)(2,1)} %wo_any.1, bf16[8,6144]{1,0:T(8,128)(2,1)} %g_any.3), custom_call_target="tpu_custom_call" | custom-call | tf_op jit(solution)/shard_map/block/pallas_call | solution.py:552
  94.8 3.2 %finish.1 = (bf16[8,6144]{1,0:T(8,128)(2,1)}, bf16[8,6144]{1,0:T(8,128)(2,1)}, f32[768,384]{1,0:T(8,128)}, f32[384,768]{1,0:T(8,128)}) custom-call(bf16[8,6144]{1,0:T(8,128)(2,1)} %x_any.3, f32[1,6144]{1,0:T(1,128)} %bitcast.2, bf16[8,6144]{1,0:T(8,128)(2,1)} %g_any.3, f32[2,4,8,1536]{3,2,1,0:T(8,128)} %get-tuple-element.7.rows_any, ...), custom_call_target="tpu_custom_call" | custom-call | tf_op jit(solution)/shard_map/finish/pallas_call | solution.py:567
